TPU v7x, 128 devices: a whole 4x4x4 slice. The times are simulated.
128 devices in a mesh: frame: 4 (over z), batch: 32 (over x, y, core).
Axes of the slice: x: 4, y: 4, z: 4, core: 2. Of those that a mesh axis runs over, the one named last changes fastest.
Arguments:
- frames: bfloat16 [32, 4, 1024, 256], P('batch', None, 'frame'), may hold values from -6 to 6
- utt_len: int32 [32, 4], P('batch'), may hold values from 103 to 1024, as said below
- token_ids: int32 [32, 4, 128], P('batch', 'frame'), may hold values from 0 to 4999
- tok_len: int32 [32, 4], P('batch', 'frame'), may hold values from 38 to 128, as said below
- step: int32 [1], replicated, may hold values from 12500 to 99999
- embed: bfloat16 [5000, 256], replicated, may hold values from -0.375 to 0.375
- norm_gain: float32 [5, 256], replicated, may hold values from 0.5 to 1.5
- norm_bias: float32 [5, 256], replicated, may hold values from -1.25 to 1.25
- attn_in: bfloat16 [3, 256, 768], replicated, may hold values from -0.375 to 0.375
- attn_in_bias: float32 [3, 512], replicated, may hold values from -1.25 to 1.25
- attn_out: bfloat16 [3, 256, 256], replicated, may hold values from -1.5 to 1.5
- attn_out_bias: float32 [3, 256], replicated, may hold values from -1.25 to 1.25
- ff_in: bfloat16 [2, 256, 2048], replicated, may hold values from -0.375 to 0.375
- ff_in_bias: float32 [2, 2048], replicated, may hold values from -1.25 to 1.25
- ff_out: bfloat16 [2, 2048, 256], replicated, may hold values from -0.125 to 0.125
- ff_out_bias: float32 [2, 256], replicated, may hold values from -1.25 to 1.25
- cotangent: bfloat16 [32, 4, 128, 256], P('batch', 'frame'), may hold values from -6 to 6
Outputs:
- dec_out: bfloat16 [32, 4, 128, 256], P('batch', 'frame')
- frames_grad: float32 [32, 4, 1024, 256], P('batch', None, 'frame')
- embed_grad: float32 [5000, 256], replicated
- norm_gain_grad: float32 [5, 256], replicated
- norm_bias_grad: float32 [5, 256], replicated
- attn_in_grad: float32 [3, 256, 768], replicated
- attn_in_bias_grad: float32 [3, 512], replicated
- attn_out_grad: float32 [3, 256, 256], replicated
- attn_out_bias_grad: float32 [3, 256], replicated
- ff_in_grad: float32 [2, 256, 2048], replicated
- ff_in_bias_grad: float32 [2, 2048], replicated
- ff_out_grad: float32 [2, 2048, 256], replicated
- ff_out_bias_grad: float32 [2, 256], replicated
Inputs may be any that keep to these rules, and one draw needn't show every extreme that they name: `utt_len`: in every group one utterance, drawn from the seed, has exactly 1024 frames. `tok_len`: in every group one transcript, drawn from the seed, has exactly 128 tokens.
All inputs are finite; a program needn't handle non-finite values.
Results may differ from a plain program's by a relative error of at most 0.018.
Values may be sent and summed in bfloat16 or wider, within the bound.
No kernel may reach another device: no remote copies, remote signals or barrier semaphores. Data moves between devices by JAX's collectives and lax.ppermute only.
A program may use at most 192 MiB of HBM per device.

v0:
```python
import functools
import math

import jax
import jax.numpy as jnp
from jax import lax
from jax.experimental import pallas as pl
from jax.experimental.pallas import tpu as pltpu
from jax.sharding import PartitionSpec as P

HEADS = 4
HEAD_DIM = 64
WARMUP = 25000
EPSILON = 1e-05
MASKED = -1e30
BF = jnp.bfloat16
F32 = jnp.float32
GELU_A = math.sqrt(2.0 / math.pi)
GELU_B = GELU_A * 0.044715
VMEM_LIMIT = 56 * 1024 * 1024


def nn(left, right):
    return lax.dot_general(left, right, (((1,), (0,)), ((), ())), preferred_element_type=F32)


def nt(left, right):
    return lax.dot_general(left, right, (((1,), (1,)), ((), ())), preferred_element_type=F32)


def normalise(states):
    average = jnp.mean(states, axis=-1, keepdims=True)
    centred = states - average
    scale = lax.rsqrt(jnp.mean(centred * centred, axis=-1, keepdims=True) + EPSILON)
    return centred * scale, scale


def norm_backward(grad, unit, scale, gain):
    grad_unit = grad * gain
    mean_grad = jnp.mean(grad_unit, axis=-1, keepdims=True)
    mean_along = jnp.mean(grad_unit * unit, axis=-1, keepdims=True)
    grad_states = scale * (grad_unit - mean_grad - unit * mean_along)
    return grad_states, col_sum(grad * unit), col_sum(grad)


def col_sum(matrix):
    return jnp.sum(matrix.astype(F32), axis=0, keepdims=True)


def gelu_value(hidden):
    inner = hidden * (GELU_A + GELU_B * (hidden * hidden))
    return hidden * (0.5 + 0.5 * jnp.tanh(inner))


def gelu_both(hidden):
    square = hidden * hidden
    bent = jnp.tanh(hidden * (GELU_A + GELU_B * square))
    half = 0.5 + 0.5 * bent
    slope = half + (0.5 * hidden) * (1.0 - bent * bent) * (GELU_A + 3.0 * GELU_B * square)
    return hidden * half, slope


def lanes_of(head):
    return slice(128 * (head // 2), 128 * (head // 2) + 128)


def rows_of(head):
    return slice(HEAD_DIM * head, HEAD_DIM * head + HEAD_DIM)


def own_lanes(pair, head):
    lane = lax.broadcasted_iota(jnp.int32, pair.shape, 1)
    mine = (lane < HEAD_DIM) if head % 2 == 0 else (lane >= HEAD_DIM)
    return jnp.where(mine, pair, jnp.zeros_like(pair))


def spare_lane(head):
    return HEAD_DIM if head % 2 == 0 else 0


def with_one(query, head):
    lane = lax.broadcasted_iota(jnp.int32, query.shape, 1)
    return jnp.where(lane == spare_lane(head), jnp.ones_like(query), query)


def with_mask(key_pair, head, length):
    lane = lax.broadcasted_iota(jnp.int32, key_pair.shape, 1)
    row = lax.broadcasted_iota(jnp.int32, key_pair.shape, 0)
    bias = jnp.where(row < length, 0.0, MASKED).astype(BF)
    return jnp.where(lane == spare_lane(head), bias, key_pair)


def layer_spec(array, layer):
    shape = (None,) + array.shape[1:]
    return pl.BlockSpec(shape, lambda i: (layer,) + (0,) * (len(shape) - 1), pipeline_mode=pl.Buffered(1))


def whole_spec(shape):
    return pl.BlockSpec(shape, lambda i: (0,) * len(shape), pipeline_mode=pl.Buffered(1))


def call(kernel, outs, args, scalars=(), scratch=(), flops=0):
    in_specs = [pl.BlockSpec(memory_space=pltpu.SMEM) for _ in scalars]
    in_specs += [layer_spec(*a) if isinstance(a, tuple) else whole_spec(a.shape) for a in args]
    args = [a[0] if isinstance(a, tuple) else a for a in args]
    size = sum(a.size * a.dtype.itemsize for a in args)
    size += sum(math.prod(s) * jnp.dtype(d).itemsize for s, d in outs)
    return pl.pallas_call(
        kernel,
        grid=(1,),
        out_shape=[jax.ShapeDtypeStruct(shape, dtype) for shape, dtype in outs],
        in_specs=in_specs,
        out_specs=[whole_spec(shape) for shape, _ in outs],
        scratch_shapes=list(scratch),
        compiler_params=pltpu.CompilerParams(vmem_limit_bytes=VMEM_LIMIT),
        cost_estimate=pl.CostEstimate(flops=flops, bytes_accessed=size, transcendentals=0),
        name=kernel.__name__,
    )(*scalars, *args)


def decoder_start(
    tok_ref, emb_ref, gain_ref, shift_ref, in_ref, in_b_ref, out_ref, out_b_ref, cross_ref,
    y1_ref, norm_c_ref, qkv_ref, ctx_t_ref, prob_ref, norm_d_ref, cross_q_ref,
):
    text = emb_ref.shape[0]
    width = emb_ref.shape[1]
    start = emb_ref[...].astype(F32) * math.sqrt(width)
    unit, _ = normalise(start)
    norm_c = (unit * gain_ref[2:3] + shift_ref[2:3]).astype(BF)
    norm_c_ref[...] = norm_c
    flat = nn(norm_c, in_ref[...])
    query = (flat[:, :width] + in_b_ref[1:2, :width]).astype(BF)
    key = flat[:, width : 2 * width].astype(BF)
    value = (flat[:, 2 * width :] + in_b_ref[1:2, width:]).astype(BF)
    qkv_ref[:, :width] = query
    qkv_ref[:, width : 2 * width] = key
    qkv_ref[:, 2 * width :] = value
    value_t = value.astype(F32).T.astype(BF)
    key_at = lax.broadcasted_iota(jnp.int32, (text, text), 0)
    query_at = lax.broadcasted_iota(jnp.int32, (text, text), 1)
    seen = jnp.logical_and(key_at <= query_at, key_at < tok_ref[0])
    scaled = query * jnp.asarray(HEAD_DIM**-0.5, BF)
    parts = []
    for head in range(HEADS):
        lanes = lanes_of(head)
        score = nt(key[:, lanes], own_lanes(scaled[:, lanes], head))
        score = jnp.where(seen, score, MASKED)
        weight = jnp.exp(score - jnp.max(score, axis=0, keepdims=True))
        prob = weight / jnp.sum(weight, axis=0, keepdims=True)
        prob_ref[head] = prob
        parts.append(nn(value_t[rows_of(head)], prob.astype(BF)))
    ctx_t = jnp.concatenate(parts, axis=0)
    ctx_t_ref[...] = ctx_t.astype(BF)
    y1 = start + nn(ctx_t.T.astype(BF), out_ref[...]) + out_b_ref[1:2]
    y1_ref[...] = y1
    unit, _ = normalise(y1)
    norm_d = (unit * gain_ref[3:4] + shift_ref[3:4]).astype(BF)
    norm_d_ref[...] = norm_d
    cross_q_ref[...] = (nn(norm_d, cross_ref[:, :width]) + in_b_ref[2:3, :width]).astype(BF)


def encoder_forward(
    len_ref, x_ref, gain_ref, shift_ref, in_ref, in_b_ref, out_ref, out_b_ref,
    w1_ref, b1_ref, w2_ref, b2_ref, cin_ref,
    qkv_ref, ctx_t_ref, lse_ref, h1_ref, mem_ref, cross_ref,
    key_aug, value_t, act,
):
    rows, width = x_ref.shape
    unit, _ = normalise(x_ref[...].astype(F32))
    norm_a = (unit * gain_ref[0:1] + shift_ref[0:1]).astype(BF)
    qkv_ref[:, :width] = (nn(norm_a, in_ref[:, :width]) + in_b_ref[0:1, :width]).astype(BF)
    key = nn(norm_a, in_ref[:, width : 2 * width]).astype(BF)
    qkv_ref[:, width : 2 * width] = key
    value = (nn(norm_a, in_ref[:, 2 * width :]) + in_b_ref[0:1, width:]).astype(BF)
    qkv_ref[:, 2 * width :] = value
    value_t[...] = value.astype(F32).T.astype(BF)
    for head in range(HEADS):
        key_aug[head] = with_mask(key[:, lanes_of(head)], head, len_ref[0])
    step = 256

    def block(index, carry):
        at = pl.multiple_of(index * step, step)
        for head in range(HEADS):
            query = qkv_ref[pl.ds(at, step), lanes_of(head)] * jnp.asarray(HEAD_DIM**-0.5, BF)
            query = with_one(own_lanes(query, head), head)
            score = nt(key_aug[head], query)
            highest = jnp.max(score, axis=0, keepdims=True)
            weight = jnp.exp(score - highest)
            total = jnp.sum(weight, axis=0, keepdims=True)
            context = nn(value_t[rows_of(head)], weight.astype(BF)) * (1.0 / total)
            ctx_t_ref[rows_of(head), pl.ds(at, step)] = context.astype(BF)
            lse_ref[head : head + 1, pl.ds(at, step)] = highest + jnp.log(total)
        return carry

    lax.fori_loop(0, rows // step, block, 0)
    context = ctx_t_ref[...].astype(F32).T.astype(BF)
    h1 = x_ref[...].astype(F32) + nn(context, out_ref[...]) + out_b_ref[0:1]
    h1_ref[...] = h1
    unit, _ = normalise(h1)
    norm_b = (unit * gain_ref[1:2] + shift_ref[1:2]).astype(BF)

    def hidden_block(index, carry):
        at = pl.multiple_of(index * step, step)
        hidden = nn(norm_b, w1_ref[:, pl.ds(at, step)]) + b1_ref[0:1, pl.ds(at, step)]
        act[:, pl.ds(at, step)] = gelu_value(hidden).astype(BF)
        return carry

    lax.fori_loop(0, w1_ref.shape[1] // step, hidden_block, 0)
    memory = (h1_ref[...] + nn(act[...], w2_ref[...]) + b2_ref[0:1]).astype(BF)
    mem_ref[...] = memory
    cross_ref[:, :width] = nn(memory, cin_ref[:, width : 2 * width]).astype(BF)
    cross_ref[:, width:] = (nn(memory, cin_ref[:, 2 * width :]) + in_b_ref[2:3, width:]).astype(BF)


def decoder_main(
    tok_ref, len_ref,
    emb_ref, y1_ref, norm_c_ref, qkv_ref, ctx_t_ref, prob_ref, norm_d_ref, cross_q_ref,
    cross_ref, mem_ref, cot_ref, gain_ref, shift_ref,
    in1_ref, out1_ref, in2_ref, out2_ref, out_b_ref, w1_ref, b1_ref, w2_ref, b2_ref,
    dec_ref, dmem_ref, y0_ref, din1_ref, din2_ref, dout1_ref, dout2_ref, dw1_ref, dw2_ref,
    small_ref, db1_ref,
    probs,
):
    text, width = emb_ref.shape
    small_ref[...] = jnp.zeros_like(small_ref)
    scaled = cross_q_ref[...] * jnp.asarray(HEAD_DIM**-0.5, BF)
    value_t = cross_ref[:, width:].astype(F32).T.astype(BF)
    parts = []
    for head in range(HEADS):
        lanes = lanes_of(head)
        key = with_mask(cross_ref[:, lanes], head, len_ref[0])
        score = nt(key, with_one(own_lanes(scaled[:, lanes], head), head))
        weight = jnp.exp(score - jnp.max(score, axis=0, keepdims=True))
        prob = weight * (1.0 / jnp.sum(weight, axis=0, keepdims=True))
        probs[head] = prob
        parts.append(nn(value_t[rows_of(head)], prob.astype(BF)))
    cross_t = jnp.concatenate(parts, axis=0)
    y2 = y1_ref[...] + nn(cross_t.T.astype(BF), out2_ref[...]) + out_b_ref[2:3]
    unit_e, scale_e = normalise(y2)
    norm_e = (unit_e * gain_ref[4:5] + shift_ref[4:5]).astype(BF)
    norm_e_t = norm_e.astype(F32).T.astype(BF)
    valid = lax.broadcasted_iota(jnp.int32, (text, 1), 0) < tok_ref[0]
    grad_low = jnp.where(valid, cot_ref[...], jnp.zeros_like(cot_ref))
    grad = grad_low.astype(F32)
    grad_low_t = grad.T.astype(BF)
    y3 = y2 + b2_ref[1:2]
    grad_norm = jnp.zeros((text, width), F32)
    chunk = 512
    for at in range(0, w1_ref.shape[1], chunk):
        part = slice(at, at + chunk)
        hidden = nn(norm_e, w1_ref[:, part]) + b1_ref[1:2, part]
        value, slope = gelu_both(hidden)
        active = value.astype(BF)
        y3 = y3 + nn(active, w2_ref[part])
        grad_hidden = (nt(grad_low, w2_ref[part]) * slope).astype(BF)
        db1_ref[:, part] = col_sum(grad_hidden)
        dw1_ref[:, part] = nn(norm_e_t, grad_hidden).astype(BF)
        dw2_ref[part] = nn(grad_low_t, active).T.astype(BF)
        grad_norm = grad_norm + nt(grad_hidden, w1_ref[:, part])
    dec_ref[...] = jnp.where(valid, y3, 0.0).astype(BF)
    small_ref[4:5] = col_sum(grad)
    grad_x, small_ref[0:1], small_ref[1:2] = norm_backward(grad_norm, unit_e, scale_e, gain_ref[4:5])
    grad = grad + grad_x
    grad_low = grad.astype(BF)
    small_ref[5:6] = col_sum(grad_low)
    dout2_ref[...] = nn(cross_t.astype(BF), grad_low).astype(BF)
    grad_ctx = nt(grad_low, out2_ref[...]).astype(BF)
    key_t = cross_ref[:, :width].astype(F32).T.astype(BF)
    mem_t = mem_ref[...].astype(F32).T.astype(BF)
    dkeys = []
    dvalues = []
    dquery = []
    for pair in range(HEADS // 2):
        dkey = 0.0
        dvalue = 0.0
        for head in (2 * pair, 2 * pair + 1):
            lanes = lanes_of(head)
            own_grad = own_lanes(grad_ctx[:, lanes], head)
            prob = probs[head]
            dprob = nt(cross_ref[:, slice(width + lanes.start, width + lanes.stop)], own_grad)
            inner = jnp.sum(dprob * prob, axis=0, keepdims=True)
            dscore = (prob * (dprob - inner)).astype(BF)
            dvalue = dvalue + nn(prob.astype(BF), own_grad)
            dkey = dkey + nn(dscore, own_lanes(scaled[:, lanes], head))
            dquery.append(nn(key_t[rows_of(head)], dscore))
        dkeys.append(dkey.astype(BF))
        dvalues.append(dvalue.astype(BF))
    dq_t = jnp.concatenate(dquery, axis=0) * HEAD_DIM**-0.5
    dq = dq_t.T.astype(BF)
    dkv = jnp.concatenate(dkeys + dvalues, axis=1)
    small_ref[6:7] = col_sum(dq)
    small_ref[7:8] = col_sum(dkv[:, width:])
    norm_d = norm_d_ref[...]
    din2_ref[:, :width] = nn(norm_d.astype(F32).T.astype(BF), dq).astype(BF)
    din2_ref[:, width:] = nn(mem_t, dkv).astype(BF)
    dmem_ref[...] = nt(dkv, in2_ref[:, width:]).astype(BF)
    unit, scale = normalise(y1_ref[...])
    grad_x, small_ref[8:9], small_ref[9:10] = norm_backward(
        nt(dq, in2_ref[:, :width]), unit, scale, gain_ref[3:4]
    )
    grad = grad + grad_x
    grad_low = grad.astype(BF)
    small_ref[10:11] = col_sum(grad_low)
    dout1_ref[...] = nn(ctx_t_ref[...], grad_low).astype(BF)
    grad_ctx = nt(grad_low, out1_ref[...]).astype(BF)
    key_t = qkv_ref[:, width : 2 * width].astype(F32).T.astype(BF)
    scaled = qkv_ref[:, :width] * jnp.asarray(HEAD_DIM**-0.5, BF)
    dkeys = []
    dvalues = []
    dquery = []
    for pair in range(HEADS // 2):
        dkey = 0.0
        dvalue = 0.0
        for head in (2 * pair, 2 * pair + 1):
            lanes = lanes_of(head)
            own_grad = own_lanes(grad_ctx[:, lanes], head)
            prob = prob_ref[head]
            dprob = nt(qkv_ref[:, slice(2 * width + lanes.start, 2 * width + lanes.stop)], own_grad)
            inner = jnp.sum(dprob * prob, axis=0, keepdims=True)
            dscore = (prob * (dprob - inner)).astype(BF)
            dvalue = dvalue + nn(prob.astype(BF), own_grad)
            dkey = dkey + nn(dscore, own_lanes(scaled[:, lanes], head))
            dquery.append(nn(key_t[rows_of(head)], dscore))
        dkeys.append(dkey.astype(BF))
        dvalues.append(dvalue.astype(BF))
    dq_t = jnp.concatenate(dquery, axis=0) * HEAD_DIM**-0.5
    dqkv = jnp.concatenate([dq_t.T.astype(BF)] + dkeys + dvalues, axis=1)
    small_ref[11:12] = col_sum(dqkv[:, :width])
    small_ref[12:13] = col_sum(dqkv[:, 2 * width :])
    din1_ref[...] = nn(norm_c_ref[...].astype(F32).T.astype(BF), dqkv).astype(BF)
    unit, scale = normalise(emb_ref[...].astype(F32) * math.sqrt(width))
    grad_x, small_ref[13:14], small_ref[14:15] = norm_backward(
        nt(dqkv, in1_ref[...]), unit, scale, gain_ref[2:3]
    )
    y0_ref[...] = ((grad + grad_x) * math.sqrt(width)).astype(BF)


def embed_backward(ids_ref, grad_ref, attn_ref, feed_ref, dec_ref, db0_ref, db1_ref, out_ref):
    text = ids_ref.shape[1]
    small = (attn_ref, feed_ref, dec_ref, db0_ref, db1_ref)
    table = out_ref.shape[0] - sum(ref.shape[0] for ref in small)
    chunk = table // 4
    for at in range(0, table, chunk):
        row = lax.broadcasted_iota(jnp.int32, (chunk, text), 0) + at
        hot = jnp.where(row == ids_ref[...], 1.0, 0.0).astype(BF)
        out_ref[at : at + chunk] = nn(hot, grad_ref[...]).astype(BF)
    out_ref[table:] = jnp.concatenate([ref[...] for ref in small], axis=0).astype(BF)


def encoder_feed_backward(
    h1_ref, dmem_ref, ctx_t_ref, gain_ref, shift_ref, w1_ref, b1_ref, w2_ref, out_ref,
    dh1_ref, dctx_ref, dw1_ref, dw2_ref, dout_ref, small_ref, db1_ref,
    grad_hid,
):
    small_ref[...] = jnp.zeros_like(small_ref)
    unit, _ = normalise(h1_ref[...])
    norm_b = unit * gain_ref[1:2] + shift_ref[1:2]
    norm_b_t = norm_b.T.astype(BF)
    norm_b = norm_b.astype(BF)
    grad_low = dmem_ref[...]
    grad_low_t = grad_low.astype(F32).T.astype(BF)
    step = 256

    def block(index, carry):
        part = pl.ds(pl.multiple_of(index * step, step), step)
        hidden = nn(norm_b, w1_ref[:, part]) + b1_ref[0:1, part]
        value, slope = gelu_both(hidden)
        grad_hidden = (nt(grad_low, w2_ref[part]) * slope).astype(BF)
        grad_hid[:, part] = grad_hidden
        db1_ref[:, part] = col_sum(grad_hidden)
        dw1_ref[:, part] = nn(norm_b_t, grad_hidden).astype(BF)
        dw2_ref[part] = nn(grad_low_t, value.astype(BF)).T.astype(BF)
        return carry

    lax.fori_loop(0, w1_ref.shape[1] // step, block, 0)
    grad = grad_low.astype(F32)
    small_ref[2:3] = col_sum(grad)
    unit, scale = normalise(h1_ref[...])
    grad_x, small_ref[0:1], small_ref[1:2] = norm_backward(
        nt(grad_hid[...], w1_ref[...]), unit, scale, gain_ref[1:2]
    )
    grad = grad + grad_x
    dh1_ref[...] = grad
    grad_low = grad.astype(BF)
    small_ref[3:4] = col_sum(grad_low)
    dout_ref[...] = nn(ctx_t_ref[...], grad_low).astype(BF)
    dctx_ref[...] = nt(grad_low, out_ref[...]).astype(BF)


def encoder_attention_backward(
    len_ref, x_ref, qkv_ref, lse_ref, dctx_ref, dh1_ref, gain_ref, shift_ref, in_ref,
    dx_ref, din_ref, small_ref,
    key_aug, key_t, dkv, dq_t, dqkv,
):
    rows, width = x_ref.shape
    small_ref[...] = jnp.zeros_like(small_ref)
    for head in range(HEADS):
        lanes = lanes_of(head)
        key_aug[head] = with_mask(qkv_ref[:, slice(width + lanes.start, width + lanes.stop)], head, len_ref[0])
    key_t[...] = qkv_ref[:, width : 2 * width].astype(F32).T.astype(BF)
    dkv[...] = jnp.zeros_like(dkv)
    step = 256

    def block(index, carry):
        at = pl.multiple_of(index * step, step)
        for head in range(HEADS):
            lanes = lanes_of(head)
            query = own_lanes(qkv_ref[pl.ds(at, step), lanes] * jnp.asarray(HEAD_DIM**-0.5, BF), head)
            score = nt(key_aug[head], with_one(query, head))
            prob = jnp.exp(score - lse_ref[head : head + 1, pl.ds(at, step)])
            own_grad = own_lanes(dctx_ref[pl.ds(at, step), lanes], head)
            dprob = nt(qkv_ref[:, slice(2 * width + lanes.start, 2 * width + lanes.stop)], own_grad)
            inner = jnp.sum(dprob * prob, axis=0, keepdims=True)
            dscore = (prob * (dprob - inner)).astype(BF)
            dkv[:, lanes] += nn(dscore, query)
            dkv[:, slice(width + lanes.start, width + lanes.stop)] += nn(prob.astype(BF), own_grad)
            dq_t[rows_of(head), pl.ds(at, step)] = nn(key_t[rows_of(head)], dscore)
        return carry

    lax.fori_loop(0, rows // step, block, 0)
    dqkv[:, :width] = (dq_t[...].T * HEAD_DIM**-0.5).astype(BF)
    dqkv[:, width:] = dkv[...].astype(BF)
    small_ref[2:3] = col_sum(dqkv[:, :width])
    small_ref[3:4] = col_sum(dqkv[:, 2 * width :])
    unit, scale = normalise(x_ref[...].astype(F32))
    norm_a = unit * gain_ref[0:1] + shift_ref[0:1]
    din_ref[...] = nn(norm_a.T.astype(BF), dqkv[...]).astype(BF)
    grad_x, small_ref[0:1], small_ref[1:2] = norm_backward(
        nt(dqkv[...], in_ref[...]), unit, scale, gain_ref[0:1]
    )
    dx_ref[...] = (dh1_ref[...] + grad_x).astype(BF)


def body(
    frames, utt_len, token_ids, tok_len, step, embed, norm_gain, norm_bias, attn_in, attn_in_bias,
    attn_out, attn_out_bias, ff_in, ff_in_bias, ff_out, ff_out_bias, cotangent,
):
    width = embed.shape[1]
    hidden = ff_in.shape[2]
    frame_count = lax.axis_size("frame")
    local_len = frames.shape[2]
    rows = local_len * frame_count
    text = token_ids.shape[2]
    my_len = lax.dynamic_slice_in_dim(utt_len[0], lax.axis_index("frame"), 1)
    my_tok = tok_len[0]
    arrived = lax.all_to_all(frames[0], "frame", split_axis=0, concat_axis=1, tiled=True)
    source = arrived.reshape(rows, width)
    ids = token_ids[0, 0]
    rows_in = embed[ids]

    y1, norm_c, dec_qkv, dec_ctx_t, dec_prob, norm_d, cross_q = call(
        decoder_start,
        [
            ((text, width), F32), ((text, width), BF), ((text, 3 * width), BF), ((width, text), BF),
            ((HEADS, text, text), F32), ((text, width), BF), ((text, width), BF),
        ],
        [
            rows_in, norm_gain, norm_bias, (attn_in, 1), attn_in_bias, (attn_out, 1),
            attn_out_bias, (attn_in, 2),
        ],
        [my_tok],
        flops=2 * text * width * width * 5,
    )
    enc_qkv, enc_ctx_t, lse, h1, memory, cross_kv = call(
        encoder_forward,
        [
            ((rows, 3 * width), BF), ((width, rows), BF), ((8, rows), F32), ((rows, width), F32),
            ((rows, width), BF), ((rows, 2 * width), BF),
        ],
        [
            source, norm_gain, norm_bias, (attn_in, 0), attn_in_bias, (attn_out, 0),
            attn_out_bias, (ff_in, 0), ff_in_bias, (ff_out, 0), ff_out_bias, (attn_in, 2),
        ],
        [my_len],
        [
            pltpu.VMEM((HEADS, rows, 128), BF), pltpu.VMEM((width, rows), BF),
            pltpu.VMEM((rows, hidden), BF),
        ],
        flops=2 * rows * width * (6 * width + 2 * rows + 2 * hidden),
    )
    (
        dec_out, dmem, y0_grad, din1, din2, dout1, dout2, dec_dw1, dec_dw2, dec_small, dec_db1,
    ) = call(
        decoder_main,
        [
            ((text, width), BF), ((rows, width), BF), ((text, width), BF),
            ((width, 3 * width), BF), ((width, 3 * width), BF), ((width, width), BF),
            ((width, width), BF), ((width, hidden), BF), ((hidden, width), BF),
            ((16, width), F32), ((1, hidden), F32),
        ],
        [
            rows_in, y1, norm_c, dec_qkv, dec_ctx_t, dec_prob, norm_d, cross_q, cross_kv, memory,
            cotangent[0, 0], norm_gain, norm_bias, (attn_in, 1), (attn_out, 1), (attn_in, 2),
            (attn_out, 2), attn_out_bias, (ff_in, 1), ff_in_bias, (ff_out, 1), ff_out_bias,
        ],
        [my_tok, my_len],
        [pltpu.VMEM((HEADS, rows, text), F32)],
        flops=2 * text * width * (6 * hidden + 7 * rows + 16 * width) + 2 * rows * width * 4 * width,
    )
    dh1, dctx, enc_dw1, enc_dw2, dout0, feed_small, enc_db1 = call(
        encoder_feed_backward,
        [
            ((rows, width), F32), ((rows, width), BF), ((width, hidden), BF), ((hidden, width), BF),
            ((width, width), BF), ((8, width), F32), ((1, hidden), F32),
        ],
        [
            h1, dmem, enc_ctx_t, norm_gain, norm_bias, (ff_in, 0), ff_in_bias, (ff_out, 0),
            (attn_out, 0),
        ],
        scratch=[pltpu.VMEM((rows, hidden), BF)],
        flops=2 * rows * width * (5 * hidden + 2 * width),
    )
    dx, din0, attn_small = call(
        encoder_attention_backward,
        [((rows, width), BF), ((width, 3 * width), BF), ((8, width), F32)],
        [source, enc_qkv, lse, dctx, dh1, norm_gain, norm_bias, (attn_in, 0)],
        [my_len],
        [
            pltpu.VMEM((HEADS, rows, 128), BF), pltpu.VMEM((width, rows), BF),
            pltpu.VMEM((rows, 2 * width), F32), pltpu.VMEM((width, rows), F32),
            pltpu.VMEM((rows, 3 * width), BF),
        ],
        flops=2 * rows * width * (5 * rows + 6 * width),
    )
    vocab = embed.shape[0]
    table = -(-vocab // 64) * 64
    (table_grad,) = call(
        embed_backward,
        [((table + 48, width), BF)],
        [
            ids[None], y0_grad, attn_small, feed_small, dec_small,
            enc_db1.reshape(-1, width), dec_db1.reshape(-1, width),
        ],
        flops=2 * table * width * text,
    )
    frames_grad = lax.all_to_all(
        dx.reshape(frame_count, local_len, width), "frame", split_axis=0, concat_axis=0, tiled=True
    ).astype(F32)[None]
    low = (table_grad, din0, din1, din2, dout0, dout1, dout2, enc_dw1, dec_dw1, enc_dw2, dec_dw2)
    summed = lax.psum(low, ("frame", "batch"))
    count_step = step[0].astype(F32)
    rate = jnp.minimum(lax.rsqrt(count_step), count_step * WARMUP ** (-1.5)) * WARMUP**0.5
    full = tuple(item.astype(F32) * rate for item in summed)
    small = full[0][table:]
    pick = lambda *at: jnp.concatenate([small[i : i + 1] for i in at])
    return (
        dec_out[None, None],
        frames_grad,
        full[0][:vocab],
        pick(0, 8, 29, 24, 16),
        pick(1, 9, 30, 25, 17),
        jnp.stack(full[1:4]),
        pick(2, 3, 27, 28, 22, 23).reshape(3, 2 * width),
        jnp.stack(full[4:7]),
        pick(11, 26, 21),
        jnp.stack(full[7:9]),
        small[32:].reshape(2, hidden),
        jnp.stack(full[9:11]),
        pick(10, 20),
    )


def solution(mesh):
    placed = (
        P("batch", None, "frame", None),
        P("batch", None),
        P("batch", "frame", None),
        P("batch", "frame"),
        P(),
        P(),
        P(),
        P(),
        P(),
        P(),
        P(),
        P(),
        P(),
        P(),
        P(),
        P(),
        P("batch", "frame", None, None),
    )
    return jax.shard_map(
        body,
        mesh=mesh,
        in_specs=placed,
        out_specs=(
            P("batch", "frame", None, None),
            P("batch", None, "frame", None),
            P(),
            P(),
            P(),
            P(),
            P(),
            P(),
            P(),
            P(),
            P(),
            P(),
            P(),
        ),
        check_vma=False,
    )
```

profile of v0, /device:TPU:1, one launch (start us, length us, event | category | flops | bytes accessed | tf_op | source)
XLA Modules:
  0.0 296.9 jit_solution(10719139180727157845)
XLA Ops:
  7.2 0.0 copy-start
  7.2 6.0 %all-to-all-start = ((bf16[4,256,256]{2,1,0:T(8,128)(2,1)}), bf16[4,256,256]{2,1,0:T(8,128)(2,1)S(1)}, u32[]{:S(2)}, u32[]{:S(2)}) async-start(bf16[4,256,256]{2,1,0:T(8,128)(2,1)} %bitcast.38), calls=%async_computation | async-start | bytes 1048576 | tf_op jit(solution)/shard_map/all_to_all | solution.py:446
  13.2 0.0 all-reduce.3.cloned.1.call-start
  13.8 1.2 constant_dynamic-slice_fusion
  15.1 0.7 fusion
  15.8 0.0 copy-done
  15.8 1.5 gather_fusion
  17.2 3.3 %decoder_start.1 = (f32[128,256]{1,0:T(8,128)}, bf16[128,256]{1,0:T(8,128)(2,1)}, bf16[128,768]{1,0:T(8,128)(2,1)}, bf16[256,128]{1,0:T(8,128)(2,1)}, f32[4,128,...) custom-call(s32[1]{0:T(128)} %bitcast.36.tok_ref, bf16[128,256]{1,0:T(8,128)(2,1)} %gather_fusion, ...), custom_call_target="tpu_custom_call" | custom-call | flops 83886080 | bytes 3689472 | tf_op jit(solution)/shard_map/decoder_start/pallas_call | solution.py:108
  20.5 0.9 all-to-all-done
  21.5 0.8 copy-done.6
  22.3 22.8 %encoder_forward.1 = (bf16[1024,768]{1,0:T(8,128)(2,1)}, bf16[256,1024]{1,0:T(8,128)(2,1)}, f32[8,1024]{1,0:T(8,128)}, f32[1024,256]{1,0:T(8,128)}, bf16[1024,25...) custom-call(s32[1]{0:T(128)} %bitcast.1.len_ref, bf16[1024,256]{1,0:T(8,128)(2,1)} %bitcast.39, f32[5,256]{1,0:T(8,128)} %gain_ref.9, ...), custom_call_target="tpu_custom_call" | custom-call | flops 4026531840 | bytes 12260352 | tf_op jit(solution)/shard_map/encoder_forward/pallas_call | solution.py:108
  45.1 13.3 %decoder_main.1 = (bf16[128,256]{1,0:T(8,128)(2,1)}, bf16[1024,256]{1,0:T(8,128)(2,1)}, bf16[128,256]{1,0:T(8,128)(2,1)}, bf16[256,768]{1,0:T(8,128)(2,1)}, bf16...) custom-call(s32[1]{0:T(128)} %bitcast.37.tok_ref, ...), custom_call_target="tpu_custom_call" | custom-call | flops 2080374784 | bytes 13753344 | tf_op jit(solution)/shard_map/decoder_main/pallas_call | solution.py:108
  58.4 0.5 broadcast.24
  58.9 1.4 reduce.7
  60.2 0.6 reshape.87.db1_ref
  60.8 17.0 %encoder_feed_backward.1 = (f32[1024,256]{1,0:T(8,128)}, bf16[1024,256]{1,0:T(8,128)(2,1)}, bf16[256,2048]{1,0:T(8,128)(2,1)}, bf16[2048,256]{1,0:T(8,128)(2,1)}...) custom-call(f32[1024,256]{1,0:T(8,128)} %get-tuple-element.59.h1_ref, ...), custom_call_target="tpu_custom_call" | custom-call | flops 5637144576 | bytes 10528768 | tf_op jit(solution)/shard_map/encoder_feed_backward/pallas_call | solution.py:108
  77.8 1.4 reduce.6
  79.2 0.6 reshape.86.db0_ref
  79.8 20.6 %encoder_attention_backward.1 = (bf16[1024,256]{1,0:T(8,128)(2,1)}, bf16[256,768]{1,0:T(8,128)(2,1)}, f32[8,256]{1,0:T(8,128)}) custom-call(s32[1]{0:T(128)} %bitcast.1.len_ref, bf16[1024,256]{1,0:T(8,128)(2,1)} %bitcast.40, bf16[1024,768]{1,0:T(8,128)(2,1)} %get-tuple-element.57.qkv_ref, f32[8,1024]{1,0:T(8,128)} %get-tuple-element.58.lse_ref, ...), custom_call_target="tpu_custom_call" | custom-call | flops 3489660928 | bytes 5818368 | tf_op jit(solution)/shard_map/encoder_attention_backward/pallas_call | solution.py:108
  100.4 3.2 %embed_backward.1 = bf16[5104,256]{1,0:T(8,128)(2,1)} custom-call(s32[1,128]{1,0:T(1,128)} %bitcast.42, bf16[128,256]{1,0:T(8,128)(2,1)} %get-tuple-element.65.grad_ref, f32[8,256]{1,0:T(8,128)} %get-tuple-element.66.attn_ref, f32[8,256]{1,0:T(8,128)} %get-tuple-element.67.feed_ref, f32[16,256]{1,0:T(8,128)} %get-tuple-element.68.dec_ref, ...), custom_call_target="tpu_custom_call" | custom-call | flops 331350016 | bytes 2728448 | tf_op jit(solution)/shard_map/embed_backward/pallas_call | solution.py:108
  103.5 0.0 all-reduce.3.cloned.1.call-update
  103.6 3.5 %all-to-all-start.1 = ((bf16[4,256,256]{2,1,0:T(8,128)(2,1)}), bf16[4,256,256]{2,1,0:T(8,128)(2,1)S(1)}, u32[]{:S(2)}, u32[]{:S(2)}) async-start(bf16[4,256,256]{2,1,0:T(8,128)(2,1)} %bitcast.8), calls=%async_computation.1 | async-start | bytes 1048576 | tf_op jit(solution)/shard_map/all_to_all | solution.py:536
  107.7 6.3 %all-to-all-done.1 = bf16[4,256,256]{2,1,0:T(8,128)(2,1)S(1)} async-done(((bf16[4,256,256]{2,1,0:T(8,128)(2,1)}), bf16[4,256,256]{2,1,0:T(8,128)(2,1)S(1)}, u32[]{:S(2)}, u32[]{:S(2)}) %all-to-all-start.1) | async-done | bytes 524320 | tf_op jit(solution)/shard_map/all_to_all | solution.py:536
  114.1 1.1 bitcast_convert_fusion
  115.1 157.0 %all-reduce.3.cloned.1.call-done = (bf16[5104,256]{1,0:T(8,128)(2,1)}, bf16[256,768]{1,0:T(8,128)(2,1)}, bf16[256,768]{1,0:T(8,128)(2,1)}, bf16[256,768]{1,0:T(8...) async-done(((bf16[5104,256]{1,0:T(8,128)(2,1)}, ...) | async-done | bytes 8380432 | tf_op jit(solution)/shard_map/psum | solution.py:540
  272.1 2.1 convert_multiply_fusion
  274.2 0.0 copy-start.8
  274.2 0.0 copy-start.7
  274.3 0.0 copy-start.9
  274.3 0.0 copy-start.10
  274.3 2.6 slice.111
  277.0 0.0 copy-done.7
  277.0 0.1 multiply_bitcast_fusion.6
  277.0 0.6 reshape.88
  277.6 0.6 reshape.89
  278.3 1.2 multiply_bitcast_fusion.4
  279.6 0.6 pad_maximum_fusion.6
  280.2 0.6 multiply_bitcast_fusion.2
  280.7 2.3 pad_maximum_fusion
  283.0 0.1 copy-done.3
  283.1 0.3 multiply_bitcast_fusion
  283.5 2.3 pad_maximum_fusion.1
  285.7 0.9 pad_maximum_fusion.3
  286.7 1.6 pad_maximum_fusion.2
  288.2 0.6 pad_maximum_fusion.5
  288.8 0.6 concatenate.17
  289.4 0.6 concatenate.16
  290.1 0.0 copy-done.1
  (19 shorter events, 0.1 us)
Async XLA Ops:
  7.2 8.6 %copy-start = (bf16[5000,256]{1,0:T(8,128)(2,1)S(1)}, bf16[5000,256]{1,0:T(8,128)(2,1)}, u32[]{:S(2)}) copy-start(bf16[5000,256]{1,0:T(8,128)(2,1)} %param.22) | copy-start | bytes 7680004
  7.2 14.3 %all-to-all-start = ((bf16[4,256,256]{2,1,0:T(8,128)(2,1)}), bf16[4,256,256]{2,1,0:T(8,128)(2,1)S(1)}, u32[]{:S(2)}, u32[]{:S(2)}) async-start(bf16[4,256,256]{2,1,0:T(8,128)(2,1)} %bitcast.38), calls=%async_computation | async-start | bytes 1048576 | tf_op jit(solution)/shard_map/all_to_all | solution.py:446
  13.2 258.9 %all-reduce.3.cloned.1.call-start = ((), (), s32[]{:S(2)}) async-start(), calls=%async_computation.2 | async-start | bytes 16760832 | tf_op jit(solution)/shard_map/psum | solution.py:540
  21.5 0.8 copy-start.6
  103.6 10.5 %all-to-all-start.1 = ((bf16[4,256,256]{2,1,0:T(8,128)(2,1)}), bf16[4,256,256]{2,1,0:T(8,128)(2,1)S(1)}, u32[]{:S(2)}, u32[]{:S(2)}) async-start(bf16[4,256,256]{2,1,0:T(8,128)(2,1)} %bitcast.8), calls=%async_computation.1 | async-start | bytes 1048576 | tf_op jit(solution)/shard_map/all_to_all | solution.py:536
  274.2 2.7 copy-start.8
  274.2 2.7 copy-start.7
  274.3 4.0 %copy-start.9 = (bf16[256,256]{1,0:T(8,128)(2,1)S(1)}, bf16[256,256]{1,0:T(8,128)(2,1)}, u32[]{:S(2)}) copy-start(bf16[256,256]{1,0:T(8,128)(2,1)} %get-tuple-element.85) | copy-start | bytes 393220
  274.3 4.0 %copy-start.10 = (bf16[256,256]{1,0:T(8,128)(2,1)S(1)}, bf16[256,256]{1,0:T(8,128)(2,1)}, u32[]{:S(2)}) copy-start(bf16[256,256]{1,0:T(8,128)(2,1)} %get-tuple-element.86) | copy-start | bytes 393220
  276.9 3.2 %copy-start.4 = (bf16[256,2048]{1,0:T(8,128)(2,1)S(1)}, bf16[256,2048]{1,0:T(8,128)(2,1)}, u32[]{:S(2)}) copy-start(bf16[256,2048]{1,0:T(8,128)(2,1)} %get-tuple-element.88) | copy-start | bytes 3145732
  276.9 3.2 %copy-start.5 = (bf16[256,2048]{1,0:T(8,128)(2,1)S(1)}, bf16[256,2048]{1,0:T(8,128)(2,1)}, u32[]{:S(2)}) copy-start(bf16[256,2048]{1,0:T(8,128)(2,1)} %get-tuple-element.89) | copy-start | bytes 3145732
  280.7 2.3 copy-start.2
  280.7 2.4 copy-start.3
  286.7 3.4 %copy-start.1 = (bf16[5000,256]{1,0:T(8,128)(2,1)S(1)}, bf16[5000,256]{1,0:T(8,128)(2,1)}, u32[]{:S(2)}) copy-start(bf16[5000,256]{1,0:T(8,128)(2,1)} %param.22) | copy-start | bytes 7680004
Sparse Core Ops, SparseCore 0:
  103.7 168.3 all-reduce.2
where the time goes:
time: 298 us; the launch traced here: 297 us
  waiting for transfers between devices  164 us (55%)
  Pallas kernels  80.1 us (27%)
  other arithmetic  17 us (6%)
  between operations  15.6 us (5%)
  local copies, waits for them, and re-layouts  10.5 us (4%)
  starting transfers between devices  9.49 us (3%)
    psum x1, waiting for transfers between devices, body(): summed = lax.psum(low, ('frame', 'batch'))  157 us
    pallas_call x6, Pallas kernels, call(): pl.pallas_call(kernel, grid=(1,), out_shape=[jax.ShapeDtypeStruct(shape,...  80.1 us
    all_to_all x1, waiting for transfers between devices, body(): lax.all_to_all(dx.reshape(frame_count, local_len, width), 'frame', split_...  6.33 us
    all_to_all x1, starting transfers between devices, body(): lax.all_to_all(frames[0], 'frame', split_axis=0, concat_axis=1, tiled=True)  6 us
  transfers between devices with their start and end apart: 3, of which 3 were waited for; matrix products, arithmetic and copies ran while one was open for 1% of the time, Pallas kernels for 1%

commit v1 on v0

--- a/solution.py
+++ b/solution.py
@@ -6,7 +6,7 @@
 from jax import lax
 from jax.experimental import pallas as pl
 from jax.experimental.pallas import tpu as pltpu
-from jax.sharding import PartitionSpec as P
+from jax.sharding import Mesh, PartitionSpec as P
 
 HEADS = 4
 HEAD_DIM = 64
@@ -18,6 +18,8 @@
 GELU_A = math.sqrt(2.0 / math.pi)
 GELU_B = GELU_A * 0.044715
 VMEM_LIMIT = 56 * 1024 * 1024
+SMALL = 32
+SPILL = 64
 
 
 def nn(left, right):
@@ -90,28 +92,36 @@
     return jnp.where(lane == spare_lane(head), bias, key_pair)
 
 
-def layer_spec(array, layer):
-    shape = (None,) + array.shape[1:]
-    return pl.BlockSpec(shape, lambda i: (layer,) + (0,) * (len(shape) - 1), pipeline_mode=pl.Buffered(1))
-
-
-def whole_spec(shape):
-    return pl.BlockSpec(shape, lambda i: (0,) * len(shape), pipeline_mode=pl.Buffered(1))
-
-
-def call(kernel, outs, args, scalars=(), scratch=(), flops=0):
-    in_specs = [pl.BlockSpec(memory_space=pltpu.SMEM) for _ in scalars]
-    in_specs += [layer_spec(*a) if isinstance(a, tuple) else whole_spec(a.shape) for a in args]
+def part_spec(shape, layers, at):
+    zeros = (0,) * (len(shape) - 1)
+    pick = (lambda i, *s: (s[at[0]][0],) + zeros) if isinstance(at, list) else (lambda i, *s: (at,) + zeros)
+    return pl.BlockSpec((layers,) + shape[1:], pick, pipeline_mode=pl.Buffered(1))
+
+
+def call(kernel, outs, args, scalars=(), scratch=(), flops=0, aliases=None):
+    in_specs = []
+    for a in args:
+        if isinstance(a, tuple) and a[1] is None:
+            in_specs.append(pl.BlockSpec(memory_space=pl.ANY))
+        elif isinstance(a, tuple):
+            in_specs.append(part_spec(a[0].shape, None, a[1]))
+        else:
+            in_specs.append(part_spec(a.shape, a.shape[0], 0))
     args = [a[0] if isinstance(a, tuple) else a for a in args]
+    out_specs = [part_spec(out[0], *(out[2:] or (out[0][0], 0))) for out in outs]
     size = sum(a.size * a.dtype.itemsize for a in args)
-    size += sum(math.prod(s) * jnp.dtype(d).itemsize for s, d in outs)
+    size += sum(math.prod(out[0]) * jnp.dtype(out[1]).itemsize for out in outs)
     return pl.pallas_call(
         kernel,
-        grid=(1,),
-        out_shape=[jax.ShapeDtypeStruct(shape, dtype) for shape, dtype in outs],
-        in_specs=in_specs,
-        out_specs=[whole_spec(shape) for shape, _ in outs],
-        scratch_shapes=list(scratch),
+        grid_spec=pltpu.PrefetchScalarGridSpec(
+            num_scalar_prefetch=len(scalars),
+            grid=(1,),
+            in_specs=in_specs,
+            out_specs=out_specs,
+            scratch_shapes=list(scratch),
+        ),
+        out_shape=[jax.ShapeDtypeStruct(out[0], out[1]) for out in outs],
+        input_output_aliases=aliases or {},
         compiler_params=pltpu.CompilerParams(vmem_limit_bytes=VMEM_LIMIT),
         cost_estimate=pl.CostEstimate(flops=flops, bytes_accessed=size, transcendentals=0),
         name=kernel.__name__,
@@ -217,11 +227,11 @@
     emb_ref, y1_ref, norm_c_ref, qkv_ref, ctx_t_ref, prob_ref, norm_d_ref, cross_q_ref,
     cross_ref, mem_ref, cot_ref, gain_ref, shift_ref,
     in1_ref, out1_ref, in2_ref, out2_ref, out_b_ref, w1_ref, b1_ref, w2_ref, b2_ref,
-    dec_ref, dmem_ref, y0_ref, din1_ref, din2_ref, dout1_ref, dout2_ref, dw1_ref, dw2_ref,
-    small_ref, db1_ref,
-    probs,
+    dec_ref, dmem_ref, early_ref, late_ref, swap_ref,
+    probs, small_ref,
 ):
     text, width = emb_ref.shape
+    blocks = w1_ref.shape[1] // width
     small_ref[...] = jnp.zeros_like(small_ref)
     scaled = cross_q_ref[...] * jnp.asarray(HEAD_DIM**-0.5, BF)
     value_t = cross_ref[:, width:].astype(F32).T.astype(BF)
@@ -253,9 +263,13 @@
         active = value.astype(BF)
         y3 = y3 + nn(active, w2_ref[part])
         grad_hidden = (nt(grad_low, w2_ref[part]) * slope).astype(BF)
-        db1_ref[:, part] = col_sum(grad_hidden)
-        dw1_ref[:, part] = nn(norm_e_t, grad_hidden).astype(BF)
-        dw2_ref[part] = nn(grad_low_t, active).T.astype(BF)
+        bias = col_sum(grad_hidden)
+        first = nn(norm_e_t, grad_hidden).astype(BF)
+        for sub in range(0, chunk, width):
+            row = (at + sub) // width
+            small_ref[16 + row : 17 + row] = bias[:, sub : sub + width]
+            early_ref[width * row : width * row + width] = first[:, sub : sub + width]
+        early_ref[width * blocks + at : width * blocks + at + chunk] = nn(grad_low_t, active).T.astype(BF)
         grad_norm = grad_norm + nt(grad_hidden, w1_ref[:, part])
     dec_ref[...] = jnp.where(valid, y3, 0.0).astype(BF)
     small_ref[4:5] = col_sum(grad)
@@ -263,7 +277,7 @@
     grad = grad + grad_x
     grad_low = grad.astype(BF)
     small_ref[5:6] = col_sum(grad_low)
-    dout2_ref[...] = nn(cross_t.astype(BF), grad_low).astype(BF)
+    early_ref[width * (2 * blocks + 3) :] = nn(cross_t.astype(BF), grad_low).astype(BF)
     grad_ctx = nt(grad_low, out2_ref[...]).astype(BF)
     key_t = cross_ref[:, :width].astype(F32).T.astype(BF)
     mem_t = mem_ref[...].astype(F32).T.astype(BF)
@@ -291,8 +305,11 @@
     small_ref[6:7] = col_sum(dq)
     small_ref[7:8] = col_sum(dkv[:, width:])
     norm_d = norm_d_ref[...]
-    din2_ref[:, :width] = nn(norm_d.astype(F32).T.astype(BF), dq).astype(BF)
-    din2_ref[:, width:] = nn(mem_t, dkv).astype(BF)
+    base = 2 * width * blocks
+    early_ref[base : base + width] = nn(norm_d.astype(F32).T.astype(BF), dq).astype(BF)
+    pairs = nn(mem_t, dkv).astype(BF)
+    early_ref[base + width : base + 2 * width] = pairs[:, :width]
+    early_ref[base + 2 * width : base + 3 * width] = pairs[:, width:]
     dmem_ref[...] = nt(dkv, in2_ref[:, width:]).astype(BF)
     unit, scale = normalise(y1_ref[...])
     grad_x, small_ref[8:9], small_ref[9:10] = norm_backward(
@@ -301,7 +318,9 @@
     grad = grad + grad_x
     grad_low = grad.astype(BF)
     small_ref[10:11] = col_sum(grad_low)
-    dout1_ref[...] = nn(ctx_t_ref[...], grad_low).astype(BF)
+    dout1 = nn(ctx_t_ref[...], grad_low).astype(BF)
+    late_ref[3 * width :] = dout1[: width - SPILL]
+    swap_ref[text + SMALL :] = dout1[width - SPILL :]
     grad_ctx = nt(grad_low, out1_ref[...]).astype(BF)
     key_t = qkv_ref[:, width : 2 * width].astype(F32).T.astype(BF)
     scaled = qkv_ref[:, :width] * jnp.asarray(HEAD_DIM**-0.5, BF)
@@ -327,31 +346,132 @@
     dqkv = jnp.concatenate([dq_t.T.astype(BF)] + dkeys + dvalues, axis=1)
     small_ref[11:12] = col_sum(dqkv[:, :width])
     small_ref[12:13] = col_sum(dqkv[:, 2 * width :])
-    din1_ref[...] = nn(norm_c_ref[...].astype(F32).T.astype(BF), dqkv).astype(BF)
+    din1 = nn(norm_c_ref[...].astype(F32).T.astype(BF), dqkv).astype(BF)
+    for part in range(3):
+        late_ref[width * part : width * part + width] = din1[:, width * part : width * part + width]
     unit, scale = normalise(emb_ref[...].astype(F32) * math.sqrt(width))
     grad_x, small_ref[13:14], small_ref[14:15] = norm_backward(
         nt(dqkv, in1_ref[...]), unit, scale, gain_ref[2:3]
     )
-    y0_ref[...] = ((grad + grad_x) * math.sqrt(width)).astype(BF)
-
-
-def embed_backward(ids_ref, grad_ref, attn_ref, feed_ref, dec_ref, db0_ref, db1_ref, out_ref):
-    text = ids_ref.shape[1]
-    small = (attn_ref, feed_ref, dec_ref, db0_ref, db1_ref)
-    table = out_ref.shape[0] - sum(ref.shape[0] for ref in small)
-    chunk = table // 4
-    for at in range(0, table, chunk):
-        row = lax.broadcasted_iota(jnp.int32, (chunk, text), 0) + at
+    swap_ref[:text] = ((grad + grad_x) * math.sqrt(width)).astype(BF)
+    swap_ref[text : text + SMALL] = small_ref[...].astype(BF)
+
+
+def early_merge(core_ref, ids_ref, early_ref, other_ref, swap_ref, swapped_ref, out_ref):
+    core = core_ref[0]
+    text = ids_ref.shape[1] // 2
+    half = other_ref.shape[0]
+    out_ref[:half] = (early_ref[...].astype(F32) + other_ref[...].astype(F32)).astype(BF)
+    grad = jnp.concatenate([swap_ref[:text], swapped_ref[:text]], axis=0)
+    chunk = half // 4
+    for at in range(0, half, chunk):
+        row = lax.broadcasted_iota(jnp.int32, (chunk, 2 * text), 0) + (at + core * half)
         hot = jnp.where(row == ids_ref[...], 1.0, 0.0).astype(BF)
-        out_ref[at : at + chunk] = nn(hot, grad_ref[...]).astype(BF)
-    out_ref[table:] = jnp.concatenate([ref[...] for ref in small], axis=0).astype(BF)
+        out_ref[half + at : half + at + chunk] = nn(hot, grad).astype(BF)
+
+    @pl.when(core == 1)
+    def _():
+        rest = swap_ref[text:].astype(F32) + swapped_ref[text:].astype(F32)
+        out_ref[2 * half - rest.shape[0] :] = rest.astype(BF)
+
+
+def late_merge(core_ref, feed_ref, feed_other_ref, attn_ref, attn_other_ref, early_ref, out_ref):
+    count = out_ref.shape[0]
+    size = early_ref.shape[1]
+    feed = feed_ref[...].astype(F32) + feed_other_ref[...].astype(F32)
+    attn = attn_ref[...].astype(F32) + attn_other_ref[...].astype(F32)
+    late = jnp.concatenate([feed.astype(BF), attn.astype(BF)], axis=0)
+    out_ref[:, size:] = late.reshape(count, -1, late.shape[1])
+    early = jnp.sum(early_ref[...].astype(F32), axis=0).astype(BF)
+    for place in range(count):
+        out_ref[place, :size] = early
+
+
+def late_split(parts_ref, early_ref, late_ref):
+    size = early_ref.shape[1]
+    early_ref[...] = parts_ref[:, :size]
+    late = jnp.sum(parts_ref[:, size:].astype(F32), axis=0).astype(BF)
+    for place in range(late_ref.shape[0]):
+        late_ref[place] = late
+
+
+def early_outputs(core_ref, rate_ref, mine_ref, other_ref, table_ref, in_ref, out_ref, w1_ref, w2_ref, rest_ref):
+    rate = rate_ref[0]
+    first = core_ref[0] == 0
+    half = mine_ref.shape[0] // 2
+    width = mine_ref.shape[1]
+    blocks = w1_ref.shape[1] // width
+
+    def rows(core, at, size):
+        mine, other = mine_ref[at : at + size], other_ref[at : at + size]
+        return jnp.where(first, mine, other) if core == 0 else jnp.where(first, other, mine)
+
+    table_ref[:half] = rows(0, half, half).astype(F32) * rate
+    rest = rows(1, half, half)
+    table_ref[half:] = rest[: table_ref.shape[0] - half].astype(F32) * rate
+    rest_ref[...] = rest[half - rest_ref.shape[0] :]
+    grads = jnp.concatenate([rows(0, 0, half), rows(1, 0, half)], axis=0).astype(F32) * rate
+    for block in range(blocks):
+        w1_ref[:, width * block : width * block + width] = grads[width * block : width * block + width]
+    w2_ref[...] = grads[width * blocks : 2 * width * blocks]
+    base = 2 * width * blocks
+    for part in range(3):
+        in_ref[:, width * part : width * part + width] = grads[base + width * part : base + width * part + width]
+    out_ref[...] = grads[base + 3 * width :]
+
+
+def late_outputs(
+    core_ref, rate_ref, mine_ref, other_ref, early_ref, in_in, out_in, w1_in, w2_in,
+    in_ref, out_ref, w1_ref, w2_ref, small_ref,
+):
+    rate = rate_ref[0]
+    first = core_ref[0] == 0
+    width = mine_ref.shape[1]
+    hidden = w2_ref.shape[0]
+    blocks = hidden // width
+    cut = (width - SPILL) // 2
+    base = hidden + 2 * width
+
+    def rows(core, at, size):
+        mine, other = mine_ref[at : at + size], other_ref[at : at + size]
+        picked = jnp.where(first, mine, other) if core == 0 else jnp.where(first, other, mine)
+        return picked.astype(F32) * rate
+
+    for block in range(blocks):
+        w1_ref[:, width * block : width * block + width] = rows(0, width * block, width)
+    w2_ref[...] = rows(1, 0, hidden)
+    in_ref[1, :, :width] = rows(0, hidden, width)
+    in_ref[1, :, width : 2 * width] = rows(0, hidden + width, width)
+    in_ref[1, :, 2 * width :] = rows(1, hidden, width)
+    out_ref[0] = rows(1, hidden + width, width)
+    out_ref[1, :cut] = rows(0, base, cut)
+    out_ref[1, cut : 2 * cut] = rows(1, base, cut)
+    out_ref[1, 2 * cut :] = early_ref[SMALL:].astype(F32) * rate
+    attn = jnp.concatenate([rows(core, base + cut, mine_ref.shape[0] - base - cut) for core in range(2)], axis=0)
+    for part in range(3):
+        in_ref[0, :, width * part : width * part + width] = attn[width * part : width * part + width]
+    small_ref[:SMALL] = attn[3 * width : 3 * width + SMALL]
+    small_ref[SMALL:] = early_ref[:SMALL].astype(F32) * rate
+
+
+def frames_back(place_ref, own_ref, next_ref, second_ref, third_ref, out_ref):
+    count = out_ref.shape[0]
+    for shift, ref in enumerate((own_ref, next_ref, second_ref, third_ref)):
+        out_ref[lax.rem(place_ref[0] + (count - shift), count)] = ref[...].astype(F32)
 
 
 def encoder_feed_backward(
-    h1_ref, dmem_ref, ctx_t_ref, gain_ref, shift_ref, w1_ref, b1_ref, w2_ref, out_ref,
-    dh1_ref, dctx_ref, dw1_ref, dw2_ref, dout_ref, small_ref, db1_ref,
+    h1_ref, dmem_ref, ctx_t_ref, gain_ref, shift_ref, w1_ref, b1_ref, w2_ref, out_ref, late_ref,
+    dh1_ref, dctx_ref, feed_ref, small_ref,
     grad_hid,
 ):
+    width = h1_ref.shape[1]
+    hidden_size = w1_ref.shape[1]
+    cut = (width - SPILL) // 2
+    feed_ref[0, hidden_size : hidden_size + 2 * width] = late_ref[: 2 * width]
+    feed_ref[1, hidden_size : hidden_size + width] = late_ref[2 * width : 3 * width]
+    feed_ref[0, hidden_size + 2 * width :] = late_ref[3 * width : 3 * width + cut]
+    feed_ref[1, hidden_size + 2 * width :] = late_ref[3 * width + cut :]
     small_ref[...] = jnp.zeros_like(small_ref)
     unit, _ = normalise(h1_ref[...])
     norm_b = unit * gain_ref[1:2] + shift_ref[1:2]
@@ -367,9 +487,9 @@
         value, slope = gelu_both(hidden)
         grad_hidden = (nt(grad_low, w2_ref[part]) * slope).astype(BF)
         grad_hid[:, part] = grad_hidden
-        db1_ref[:, part] = col_sum(grad_hidden)
-        dw1_ref[:, part] = nn(norm_b_t, grad_hidden).astype(BF)
-        dw2_ref[part] = nn(grad_low_t, value.astype(BF)).T.astype(BF)
+        small_ref[pl.ds(8 + index, 1)] = col_sum(grad_hidden)
+        feed_ref[0, part] = nn(norm_b_t, grad_hidden).astype(BF)
+        feed_ref[1, part] = nn(grad_low_t, value.astype(BF)).T.astype(BF)
         return carry
 
     lax.fori_loop(0, w1_ref.shape[1] // step, block, 0)
@@ -383,17 +503,18 @@
     dh1_ref[...] = grad
     grad_low = grad.astype(BF)
     small_ref[3:4] = col_sum(grad_low)
-    dout_ref[...] = nn(ctx_t_ref[...], grad_low).astype(BF)
+    feed_ref[1, hidden_size + width : hidden_size + 2 * width] = nn(ctx_t_ref[...], grad_low).astype(BF)
     dctx_ref[...] = nt(grad_low, out_ref[...]).astype(BF)
 
 
 def encoder_attention_backward(
-    len_ref, x_ref, qkv_ref, lse_ref, dctx_ref, dh1_ref, gain_ref, shift_ref, in_ref,
-    dx_ref, din_ref, small_ref,
-    key_aug, key_t, dkv, dq_t, dqkv,
+    len_ref, x_ref, qkv_ref, lse_ref, dctx_ref, dh1_ref, gain_ref, shift_ref, in_ref, feed_small_ref,
+    dx_ref, attn_ref,
+    key_aug, key_t, dkv, dq_t, dqkv, small_ref,
 ):
     rows, width = x_ref.shape
     small_ref[...] = jnp.zeros_like(small_ref)
+    small_ref[8:24] = feed_small_ref[...]
     for head in range(HEADS):
         lanes = lanes_of(head)
         key_aug[head] = with_mask(qkv_ref[:, slice(width + lanes.start, width + lanes.stop)], head, len_ref[0])
@@ -424,29 +545,50 @@
     small_ref[3:4] = col_sum(dqkv[:, 2 * width :])
     unit, scale = normalise(x_ref[...].astype(F32))
     norm_a = unit * gain_ref[0:1] + shift_ref[0:1]
-    din_ref[...] = nn(norm_a.T.astype(BF), dqkv[...]).astype(BF)
+    din = nn(norm_a.T.astype(BF), dqkv[...]).astype(BF)
+    for part in range(3):
+        attn_ref[width * part : width * part + width] = din[:, width * part : width * part + width]
     grad_x, small_ref[0:1], small_ref[1:2] = norm_backward(
         nt(dqkv[...], in_ref[...]), unit, scale, gain_ref[0:1]
     )
     dx_ref[...] = (dh1_ref[...] + grad_x).astype(BF)
+    attn_ref[3 * width :] = jnp.zeros_like(attn_ref[3 * width :])
+    attn_ref[3 * width : 3 * width + SMALL] = small_ref[...].astype(BF)
+
+
+def swap_cores(array):
+    return lax.ppermute(array, "core", [(0, 1), (1, 0)])
+
+
+def other_half(halves, core):
+    return swap_cores(lax.dynamic_index_in_dim(halves, 1 - core, keepdims=False))
 
 
 def body(
     frames, utt_len, token_ids, tok_len, step, embed, norm_gain, norm_bias, attn_in, attn_in_bias,
     attn_out, attn_out_bias, ff_in, ff_in_bias, ff_out, ff_out_bias, cotangent,
 ):
-    width = embed.shape[1]
+    ring = ("frame", "pair")
+    devices = lax.axis_size(ring)
+    core = lax.axis_index("core")
+    core_at = core[None]
+    frame_at = lax.axis_index("frame")
+    vocab, width = embed.shape
     hidden = ff_in.shape[2]
     frame_count = lax.axis_size("frame")
     local_len = frames.shape[2]
     rows = local_len * frame_count
     text = token_ids.shape[2]
-    my_len = lax.dynamic_slice_in_dim(utt_len[0], lax.axis_index("frame"), 1)
+    my_len = lax.dynamic_slice_in_dim(utt_len[0], frame_at, 1)
     my_tok = tok_len[0]
     arrived = lax.all_to_all(frames[0], "frame", split_axis=0, concat_axis=1, tiled=True)
     source = arrived.reshape(rows, width)
     ids = token_ids[0, 0]
+    both_ids = jnp.concatenate([ids, swap_cores(ids)])[None]
     rows_in = embed[ids]
+    count_step = step[0].astype(F32)
+    rate = jnp.minimum(lax.rsqrt(count_step), count_step * WARMUP ** (-1.5)) * WARMUP**0.5
+    rate = rate[None]
 
     y1, norm_c, dec_qkv, dec_ctx_t, dec_prob, norm_d, cross_q = call(
         decoder_start,
@@ -478,15 +620,11 @@
         ],
         flops=2 * rows * width * (6 * width + 2 * rows + 2 * hidden),
     )
-    (
-        dec_out, dmem, y0_grad, din1, din2, dout1, dout2, dec_dw1, dec_dw2, dec_small, dec_db1,
-    ) = call(
+    dec_out, dmem, early, late, swap = call(
         decoder_main,
         [
-            ((text, width), BF), ((rows, width), BF), ((text, width), BF),
-            ((width, 3 * width), BF), ((width, 3 * width), BF), ((width, width), BF),
-            ((width, width), BF), ((width, hidden), BF), ((hidden, width), BF),
-            ((16, width), F32), ((1, hidden), F32),
+            ((text, width), BF), ((rows, width), BF), ((4 * width + 2 * hidden, width), BF),
+            ((4 * width - SPILL, width), BF), ((text + SMALL + SPILL, width), BF),
         ],
         [
             rows_in, y1, norm_c, dec_qkv, dec_ctx_t, dec_prob, norm_d, cross_q, cross_kv, memory,
@@ -494,110 +632,139 @@
             (attn_out, 2), attn_out_bias, (ff_in, 1), ff_in_bias, (ff_out, 1), ff_out_bias,
         ],
         [my_tok, my_len],
-        [pltpu.VMEM((HEADS, rows, text), F32)],
+        [pltpu.VMEM((HEADS, rows, text), F32), pltpu.VMEM((SMALL, width), F32)],
         flops=2 * text * width * (6 * hidden + 7 * rows + 16 * width) + 2 * rows * width * 4 * width,
     )
-    dh1, dctx, enc_dw1, enc_dw2, dout0, feed_small, enc_db1 = call(
+    swapped = swap_cores(swap)
+    half = early.shape[0] // 2
+    early = early.reshape(2, half, width)
+    (early_sum,) = call(
+        early_merge,
+        [((2 * half, width), BF)],
+        [both_ids, (early, [0]), other_half(early, core), swap, swapped],
+        [core_at],
+        flops=4 * half * width * text,
+    )
+    early_sum, dmem = lax.optimization_barrier((early_sum, dmem))
+    early_parts = lax.all_to_all(
+        early_sum.reshape(devices, -1, width), ring, split_axis=0, concat_axis=0, tiled=True
+    )
+    early_own = jnp.sum(early_parts.astype(F32), axis=0).astype(BF)
+
+    dh1, dctx, feed, feed_small = call(
         encoder_feed_backward,
         [
-            ((rows, width), F32), ((rows, width), BF), ((width, hidden), BF), ((hidden, width), BF),
-            ((width, width), BF), ((8, width), F32), ((1, hidden), F32),
+            ((rows, width), F32), ((rows, width), BF), ((2, (5 * width - SPILL) // 2 + hidden, width), BF),
+            ((16, width), F32),
         ],
         [
             h1, dmem, enc_ctx_t, norm_gain, norm_bias, (ff_in, 0), ff_in_bias, (ff_out, 0),
-            (attn_out, 0),
+            (attn_out, 0), late,
         ],
         scratch=[pltpu.VMEM((rows, hidden), BF)],
         flops=2 * rows * width * (5 * hidden + 2 * width),
     )
-    dx, din0, attn_small = call(
+    feed_other = other_half(feed, core)
+    dx, attn = call(
         encoder_attention_backward,
-        [((rows, width), BF), ((width, 3 * width), BF), ((8, width), F32)],
-        [source, enc_qkv, lse, dctx, dh1, norm_gain, norm_bias, (attn_in, 0)],
+        [((rows, width), BF), ((3 * width + 2 * SMALL, width), BF)],
+        [source, enc_qkv, lse, dctx, dh1, norm_gain, norm_bias, (attn_in, 0), feed_small],
         [my_len],
         [
             pltpu.VMEM((HEADS, rows, 128), BF), pltpu.VMEM((width, rows), BF),
             pltpu.VMEM((rows, 2 * width), F32), pltpu.VMEM((width, rows), F32),
-            pltpu.VMEM((rows, 3 * width), BF),
+            pltpu.VMEM((rows, 3 * width), BF), pltpu.VMEM((SMALL, width), F32),
         ],
         flops=2 * rows * width * (5 * rows + 6 * width),
     )
-    vocab = embed.shape[0]
-    table = -(-vocab // 64) * 64
-    (table_grad,) = call(
-        embed_backward,
-        [((table + 48, width), BF)],
-        [
-            ids[None], y0_grad, attn_small, feed_small, dec_small,
-            enc_db1.reshape(-1, width), dec_db1.reshape(-1, width),
-        ],
-        flops=2 * table * width * text,
-    )
-    frames_grad = lax.all_to_all(
-        dx.reshape(frame_count, local_len, width), "frame", split_axis=0, concat_axis=0, tiled=True
-    ).astype(F32)[None]
-    low = (table_grad, din0, din1, din2, dout0, dout1, dout2, enc_dw1, dec_dw1, enc_dw2, dec_dw2)
-    summed = lax.psum(low, ("frame", "batch"))
-    count_step = step[0].astype(F32)
-    rate = jnp.minimum(lax.rsqrt(count_step), count_step * WARMUP ** (-1.5)) * WARMUP**0.5
-    full = tuple(item.astype(F32) * rate for item in summed)
-    small = full[0][table:]
+    attn = attn.reshape(2, -1, width)
+    late_half = feed.shape[1] + attn.shape[1]
+    (mixed,) = call(
+        late_merge,
+        [((devices, (2 * half + late_half) // devices, width), BF)],
+        [(feed, [0]), feed_other, (attn, [0]), other_half(attn, core), early_parts],
+        [core_at],
+    )
+    mixed = lax.all_to_all(mixed, ring, split_axis=0, concat_axis=0, tiled=True)
+    chunks = dx.reshape(frame_count, local_len, width)
+    moved = []
+    for shift in range(frame_count):
+        target = lax.rem(frame_at + shift, frame_count)
+        chunk = lax.dynamic_index_in_dim(chunks, target, keepdims=False)
+        if shift:
+            chunk = lax.ppermute(chunk, "frame", [(i, (i + shift) % frame_count) for i in range(frame_count)])
+        moved.append(chunk)
+    (frames_grad,) = call(
+        frames_back, [((frame_count, local_len, width), F32)], moved, [frame_at[None]]
+    )
+    mixed, frames_grad = lax.optimization_barrier((mixed, frames_grad))
+    early_mine, late_own = call(
+        late_split,
+        [((devices, 2 * half // devices, width), BF), ((devices, late_half // devices, width), BF)],
+        [mixed],
+    )
+    early_mine = early_mine.reshape(2 * half, width)
+    early_other = swap_cores(early_mine)
+    late_mine = lax.all_to_all(late_own, ring, split_axis=0, concat_axis=0, tiled=True)
+    in_shape = (3, width, 3 * width)
+    out_shape = (3, width, width)
+    w1_shape = (2, width, hidden)
+    w2_shape = (2, hidden, width)
+    table_grad, in_grad, out_grad, w1_grad, w2_grad, early_rest = call(
+        early_outputs,
+        [
+            ((vocab, width), F32), (in_shape, F32, None, 2), (out_shape, F32, None, 2),
+            (w1_shape, F32, None, 1), (w2_shape, F32, None, 1), ((SMALL + SPILL, width), BF),
+        ],
+        [early_mine, early_other],
+        [core_at, rate],
+    )
+    late_mine, early_rest = lax.optimization_barrier((late_mine, early_rest))
+    late_mine = late_mine.reshape(late_half, width)
+    late_other = swap_cores(late_mine)
+
+    in_grad, out_grad, w1_grad, w2_grad, small = call(
+        late_outputs,
+        [
+            (in_shape, F32, 2, 0), (out_shape, F32, 2, 0), (w1_shape, F32, None, 0),
+            (w2_shape, F32, None, 0), ((2 * SMALL, width), F32),
+        ],
+        [
+            late_mine, late_other, early_rest, (in_grad, None), (out_grad, None), (w1_grad, None),
+            (w2_grad, None),
+        ],
+        [core_at, rate],
+        aliases={5: 0, 6: 1, 7: 2, 8: 3},
+    )
     pick = lambda *at: jnp.concatenate([small[i : i + 1] for i in at])
+    dec = lambda i: SMALL + i
+    bias = lambda at: small[at : at + hidden // width].reshape(1, hidden)
     return (
         dec_out[None, None],
-        frames_grad,
-        full[0][:vocab],
-        pick(0, 8, 29, 24, 16),
-        pick(1, 9, 30, 25, 17),
-        jnp.stack(full[1:4]),
-        pick(2, 3, 27, 28, 22, 23).reshape(3, 2 * width),
-        jnp.stack(full[4:7]),
-        pick(11, 26, 21),
-        jnp.stack(full[7:9]),
-        small[32:].reshape(2, hidden),
-        jnp.stack(full[9:11]),
-        pick(10, 20),
+        frames_grad[None],
+        table_grad,
+        pick(0, 8, dec(13), dec(8), dec(0)),
+        pick(1, 9, dec(14), dec(9), dec(1)),
+        in_grad,
+        pick(2, 3, dec(11), dec(12), dec(6), dec(7)).reshape(3, 2 * width),
+        out_grad,
+        pick(11, dec(10), dec(5)),
+        w1_grad,
+        jnp.concatenate([bias(16), bias(dec(16))]),
+        w2_grad,
+        pick(10, dec(4)),
     )
 
 
 def solution(mesh):
+    groups = ("pair", "core")
+    frames, batch = mesh.devices.shape
+    split = Mesh(mesh.devices.reshape(frames, batch // 2, 2), ("frame",) + groups)
     placed = (
-        P("batch", None, "frame", None),
-        P("batch", None),
-        P("batch", "frame", None),
-        P("batch", "frame"),
-        P(),
-        P(),
-        P(),
-        P(),
-        P(),
-        P(),
-        P(),
-        P(),
-        P(),
-        P(),
-        P(),
-        P(),
-        P("batch", "frame", None, None),
-    )
-    return jax.shard_map(
-        body,
-        mesh=mesh,
-        in_specs=placed,
-        out_specs=(
-            P("batch", "frame", None, None),
-            P("batch", None, "frame", None),
-            P(),
-            P(),
-            P(),
-            P(),
-            P(),
-            P(),
-            P(),
-            P(),
-            P(),
-            P(),
-            P(),
-        ),
-        check_vma=False,
-    )
+        P(groups, None, "frame", None),
+        P(groups, None),
+        P(groups, "frame", None),
+        P(groups, "frame"),
+    ) + (P(),) * 12 + (P(groups, "frame", None, None),)
+    results = (P(groups, "frame", None, None), P(groups, None, "frame", None)) + (P(),) * 11
+    return jax.shard_map(body, mesh=split, in_specs=placed, out_specs=results, check_vma=False)

time: 298 us -> 247 us (0.83)
  waiting for transfers between devices: 164 us -> 72.1 us
  starting transfers between devices: 9.49 us -> 45.3 us
  Pallas kernels: 80.1 us -> 106 us
  other arithmetic: 17 us -> 3.05 us
  between operations: 15.6 us -> 2.15 us
  local copies, waits for them, and re-layouts: 10.5 us -> 17.1 us
    psum x1 -> x0, waiting for transfers between devices: 157 us -> none  [body(): summed = lax.psum(low, ('frame', 'batch'))]
    ppermute x0 -> x10, waiting for transfers between devices: none -> 55.1 us  [the longest x3 48.3 us: body(): lax.ppermute(chunk, 'frame', [(i, (i + shift) % frame_count) for i in ran...]
    all_to_all x1 -> x3, starting transfers between devices: 3.48 us -> 30 us  [the longest x1 10.7 us: body(): lax.all_to_all(late_own, ring, split_axis=0, concat_axis=0, tiled=True)]
    pallas_call x6 -> x11, Pallas kernels: 80.1 us -> 106 us  [call(): pl.pallas_call(kernel, grid_spec=pltpu.PrefetchScalarGridSpec(num_scalar_...]
    all_to_all x1 -> x3, waiting for transfers between devices: 6.33 us -> 16.1 us  [the longest x1 16.1 us: body(): lax.all_to_all(late_own, ring, split_axis=0, concat_axis=0, tiled=True)]
    another operation x10 -> x0, other arithmetic: 9.32 us -> none  [the longest x3 2.85 us: body(): jnp.stack(full[1:4])]
    ppermute x0 -> x10, starting transfers between devices: none -> 9.29 us  [the longest x7 6.15 us: swap_cores(): return lax.ppermute(array, 'core', [(0, 1), (1, 0)])]
    unnamed x22 -> x31, local copies, waits for them, and re-layouts: 0.91 us -> 6.3 us
  transfers between devices with their start and end apart: 3 -> 14, of which waited for: 3 -> 7; matrix products, arithmetic and copies ran while one was open for 1% -> 3% of each run, Pallas kernels for 1% -> 20%
where the time goes in v1:
time: 247 us; the launch traced here: 246 us
  Pallas kernels  106 us (43%)
  waiting for transfers between devices  72.1 us (29%)
  starting transfers between devices  45.3 us (18%)
  local copies, waits for them, and re-layouts  17.1 us (7%)
  other arithmetic  3.05 us (1%)
    pallas_call x11, Pallas kernels, call(): pl.pallas_call(kernel, grid_spec=pltpu.PrefetchScalarGridSpec(num_scalar_...  106 us
    ppermute x3, waiting for transfers between devices, body(): lax.ppermute(chunk, 'frame', [(i, (i + shift) % frame_count) for i in ran...  48.3 us
    all_to_all x1, waiting for transfers between devices, body(): lax.all_to_all(late_own, ring, split_axis=0, concat_axis=0, tiled=True)  16.1 us
    all_to_all x1, starting transfers between devices, body(): lax.all_to_all(late_own, ring, split_axis=0, concat_axis=0, tiled=True)  10.7 us
    all_to_all x1, starting transfers between devices, body(): mixed = lax.all_to_all(mixed, ring, split_axis=0, concat_axis=0, tiled=True)  10.4 us
    all_to_all x1, starting transfers between devices, body(): lax.all_to_all(early_sum.reshape(devices, -1, width), ring, split_axis=0,...  8.95 us
    ppermute x7, waiting for transfers between devices, swap_cores(): return lax.ppermute(array, 'core', [(0, 1), (1, 0)])  6.81 us
    unnamed x31, local copies, waits for them, and re-layouts  6.3 us
  transfers between devices with their start and end apart: 14, of which 7 were waited for; matrix products, arithmetic and copies ran while one was open for 3% of the time, Pallas kernels for 20%

profile of v1, /device:TPU:1, one launch (start us, length us, event | category | flops | bytes accessed | tf_op | source)
XLA Modules:
  0.0 245.8 jit_solution(6015380380628716520)
XLA Ops:
  0.7 6.0 %all-to-all-start = ((bf16[4,256,256]{2,1,0:T(8,128)(2,1)}), bf16[4,256,256]{2,1,0:T(8,128)(2,1)S(1)}, u32[]{:S(2)}, u32[]{:S(2)}) async-start(bf16[4,256,256]{2,1,0:T(8,128)(2,1)} %bitcast.55), calls=%async_computation | async-start | bytes 1048576 | tf_op jit(solution)/shard_map/all_to_all | solution.py:584
  7.3 1.2 constant_dynamic-slice_fusion
  8.6 0.7 fusion
  9.2 1.5 gather_fusion
  10.7 3.3 %decoder_start.1 = (f32[128,256]{1,0:T(8,128)}, bf16[128,256]{1,0:T(8,128)(2,1)}, bf16[128,768]{1,0:T(8,128)(2,1)}, bf16[256,128]{1,0:T(8,128)(2,1)}, f32[4,128,...) custom-call(s32[1]{0:T(128)} %bitcast.43.tok_ref, bf16[128,256]{1,0:T(8,128)(2,1)} %gather_fusion, ...), custom_call_target="tpu_custom_call" | custom-call | flops 83886080 | bytes 3689472 | tf_op jit(solution)/shard_map/decoder_start/pallas_call | solution.py:114
  14.0 0.9 all-to-all-done
  14.9 0.8 copy-done.5
  15.7 22.8 %encoder_forward.1 = (bf16[1024,768]{1,0:T(8,128)(2,1)}, bf16[256,1024]{1,0:T(8,128)(2,1)}, f32[8,1024]{1,0:T(8,128)}, f32[1024,256]{1,0:T(8,128)}, bf16[1024,25...) custom-call(s32[1]{0:T(128)} %bitcast.1.len_ref, bf16[1024,256]{1,0:T(8,128)(2,1)} %bitcast.56, f32[5,256]{1,0:T(8,128)} %gain_ref.9, ...), custom_call_target="tpu_custom_call" | custom-call | flops 4026531840 | bytes 12260352 | tf_op jit(solution)/shard_map/encoder_forward/pallas_call | solution.py:114
  38.6 13.7 %decoder_main.1 = (bf16[128,256]{1,0:T(8,128)(2,1)}, bf16[1024,256]{1,0:T(8,128)(2,1)}, bf16[5120,256]{1,0:T(8,128)(2,1)}, bf16[960,256]{1,0:T(8,128)(2,1)}, bf16[224,256]{1,0:T(8,128)(2,1)}) custom-call(s32[1]{0:T(128)} %bitcast.44.tok_ref, s32[1]{0:T(128)} %bitcast.1.len_ref, bf16[128,256]{1,0:T(8,128)(2,1)} %gather_fusion, ...), custom_call_target="tpu_custom_call" | custom-call | flops 2080374784 | bytes 13745152 | tf_op jit(solution)/shard_map/decoder_main/pallas_call | solution.py:114
  52.2 1.4 dynamic-slice_bitcast_fusion.1
  53.7 2.2 collective-permute-start.1
  56.4 2.3 collective-permute-done
  59.3 0.6 copy-done.12
  60.4 4.4 %early_merge.1 = bf16[5120,256]{1,0:T(8,128)(2,1)} custom-call(s32[1]{0:T(128)} %bitcast.8.core_ref, s32[1,256]{1,0:T(1,128)} %bitcast.62, bf16[2,2560,256]{2,1,0:T(8,128)(2,1)} %bitcast.49, bf16[2560,256]{1,0:T(8,128)(2,1)} %copy-done.4, bf16[224,256]{1,0:T(8,128)(2,1)} %get-tuple-element.68.swap_ref, bf16[224,256]{1,0:T(8,128)(2,1)} %copy-done.12), custom_call_target="tpu_custom_call" | custom-call | flops 335544320 | bytes 6784000 | tf_op jit(solution)/shard_map/early_merge/pallas_call | solution.py:114
  64.8 9.0 %all-to-all-start.1 = ((bf16[64,80,256]{2,1,0:T(8,128)(2,1)}), bf16[64,80,256]{2,1,0:T(8,128)(2,1)}, u32[]{:S(2)}, u32[]{:S(2)}) async-start(bf16[64,80,256]{2,1,0:T(8,128)(2,1)} %bitcast.45), calls=%async_computation.1 | async-start | bytes 5242880 | tf_op jit(solution)/shard_map/all_to_all | solution.py:649
  73.8 17.3 %encoder_feed_backward.1 = (f32[1024,256]{1,0:T(8,128)}, bf16[1024,256]{1,0:T(8,128)(2,1)}, bf16[2,2656,256]{2,1,0:T(8,128)(2,1)}, f32[16,256]{1,0:T(8,128)}) custom-call(f32[1024,256]{1,0:T(8,128)} %get-tuple-element.66.h1_ref, bf16[1024,256]{1,0:T(8,128)(2,1)} %get-tuple-element.70.dmem_ref, bf16[256,1024]{1,0:T(8,128)(2,1)} %get-tuple-element.71.ctx_t_ref, ...), custom_call_target="tpu_custom_call" | custom-call | flops 5637144576 | bytes 11511808 | tf_op jit(solution)/shard_map/encoder_feed_backward/pallas_call | solution.py:114
  91.1 1.4 dynamic-slice_bitcast_fusion
  92.5 0.7 collective-permute-start.3
  93.2 20.9 %encoder_attention_backward.1 = (bf16[1024,256]{1,0:T(8,128)(2,1)}, bf16[832,256]{1,0:T(8,128)(2,1)}) custom-call(s32[1]{0:T(128)} %bitcast.1.len_ref, bf16[1024,256]{1,0:T(8,128)(2,1)} %bitcast.57, bf16[1024,768]{1,0:T(8,128)(2,1)} %get-tuple-element.74.qkv_ref, f32[8,1024]{1,0:T(8,128)} %get-tuple-element.75.lse_ref, ...), custom_call_target="tpu_custom_call" | custom-call | flops 3489660928 | bytes 5859328 | tf_op jit(solution)/shard_map/encoder_attention_backward/pallas_call | solution.py:114
  114.1 0.9 dynamic-slice_bitcast_fusion.2
  115.2 1.4 collective-permute-done.4.attn_other_ref
  116.6 0.7 copy-done.7
  117.3 5.7 %late_merge.1 = bf16[64,128,256]{2,1,0:T(8,128)(2,1)} custom-call(s32[1]{0:T(128)} %bitcast.8.core_ref, bf16[2,2656,256]{2,1,0:T(8,128)(2,1)} %get-tuple-element.73.feed_ref, bf16[2656,256]{1,0:T(8,128)(2,1)} %collective-permute-done.3.feed_other_ref, bf16[2,416,256]{2,1,0:T(8,128)(2,1)} %bitcast.54, bf16[416,256]{1,0:T(8,128)(2,1)} %copy-done.7, ...), custom_call_target="tpu_custom_call" | custom-call | bytes 11534336 | tf_op jit(solution)/shard_map/late_merge/pallas_call | solution.py:114
  122.9 10.4 %all-to-all-start.2 = ((bf16[64,128,256]{2,1,0:T(8,128)(2,1)}), bf16[64,128,256]{2,1,0:T(8,128)(2,1)}, u32[]{:S(2)}, u32[]{:S(2)}) async-start(bf16[64,128,256]{2,1,0:T(8,128)(2,1)} %late_merge.1), calls=%async_computation.2 | async-start | bytes 8388608 | tf_op jit(solution)/shard_map/all_to_all | solution.py:688
  133.4 0.7 dynamic-slice_bitcast_fusion.3
  134.1 2.1 collective-permute-start.7
  136.6 0.7 collective-permute-start.5
  137.3 32.9 %collective-permute-done.7.third_ref = bf16[256,256]{1,0:T(8,128)(2,1)S(1)} collective-permute-done((bf16[256,256]{1,0:T(8,128)(2,1)S(1)}, bf16[256,256]{1,0:T(8,128)(2,1)S(1)}, u32[]{:S(2)}, u32[]{:S(2)}) %collective-permute-start.7) | collective-permute-done | bytes 131104 | tf_op jit(solution)/shard_map/ppermute | solution.py:695
  170.2 15.4 %collective-permute-done.5.next_ref = bf16[256,256]{1,0:T(8,128)(2,1)S(1)} collective-permute-done((bf16[256,256]{1,0:T(8,128)(2,1)S(1)}, bf16[256,256]{1,0:T(8,128)(2,1)S(1)}, u32[]{:S(2)}, u32[]{:S(2)}) %collective-permute-start.5) | collective-permute-done | bytes 131104 | tf_op jit(solution)/shard_map/ppermute | solution.py:695
  185.5 0.6 copy-done.10
  186.2 2.1 frames_back.1
  188.3 4.4 %late_split.1 = (bf16[64,80,256]{2,1,0:T(8,128)(2,1)}, bf16[64,48,256]{2,1,0:T(8,128)(2,1)}) custom-call(bf16[64,128,256]{2,1,0:T(8,128)(2,1)} %all-to-all-done.2.parts_ref), custom_call_target="tpu_custom_call" | custom-call | bytes 8388608 | tf_op jit(solution)/shard_map/late_split/pallas_call | solution.py:114
  192.7 1.0 collective-permute-start.8
  193.7 10.7 %all-to-all-start.3 = ((bf16[64,48,256]{2,1,0:T(8,128)(2,1)}), bf16[64,48,256]{2,1,0:T(8,128)(2,1)S(1)}, u32[]{:S(2)}, u32[]{:S(2)}) async-start(bf16[64,48,256]{2,1,0:T(8,128)(2,1)} %get-tuple-element.86), calls=%async_computation.3 | async-start | bytes 3145728 | tf_op jit(solution)/shard_map/all_to_all | solution.py:708
  205.0 6.7 %early_outputs.1 = (f32[5000,256]{1,0:T(8,128)}, f32[3,256,768]{2,1,0:T(8,128)}, f32[3,256,256]{2,1,0:T(8,128)}, f32[2,256,2048]{2,1,0:T(8,128)}, f32[2,2048,256]{2,1,0:T(8,128)}, /*index=5*/bf16[96,256]{1,0:T(8,128)(2,1)}) custom-call(s32[1]{0:T(128)} %bitcast.8.core_ref, f32[1]{0:T(128)S(6)} %mul.9.rate_ref, bf16[5120,256]{1,0:T(8,128)(2,1)} %bitcast.51, ...), custom_call_target="tpu_custom_call" | custom-call | bytes 21946368 | tf_op jit(solution)/shard_map/early_outputs/pallas_call | solution.py:114
  211.8 16.1 %all-to-all-done.3 = bf16[64,48,256]{2,1,0:T(8,128)(2,1)S(1)} async-done(((bf16[64,48,256]{2,1,0:T(8,128)(2,1)}), bf16[64,48,256]{2,1,0:T(8,128)(2,1)S(1)}, u32[]{:S(2)}, u32[]{:S(2)}) %all-to-all-start.3) | async-done | bytes 1572896 | tf_op jit(solution)/shard_map/all_to_all | solution.py:708
  227.8 1.2 copy-done.2
  229.0 1.6 collective-permute-start.9
  230.6 3.0 %collective-permute-done.9.other_ref = bf16[3072,256]{1,0:T(8,128)(2,1)S(1)} collective-permute-done((bf16[3072,256]{1,0:T(8,128)(2,1)S(1)}, bf16[3072,256]{1,0:T(8,128)(2,1)S(1)}, u32[]{:S(2)}, u32[]{:S(2)}) %collective-permute-start.9) | collective-permute-done | bytes 1572896 | tf_op jit(solution)/shard_map/ppermute | solution.py:560
  233.7 1.2 copy-done.3
  234.8 4.9 %late_outputs.1 = (f32[3,256,768]{2,1,0:T(8,128)}, f32[3,256,256]{2,1,0:T(8,128)}, f32[2,256,2048]{2,1,0:T(8,128)}, f32[2,2048,256]{2,1,0:T(8,128)}, f32[64,256]{1,0:T(8,128)}) custom-call(s32[1]{0:T(128)} %bitcast.8.core_ref, f32[1]{0:T(128)S(6)} %mul.9.rate_ref, ...), custom_call_target="tpu_custom_call", output_to_operand_aliasing={{0}: (5, {}), {1}: (6, {}), {2}: (7, {}), {3}: (8, {})} | custom-call | bytes 26329088 | tf_op jit(solution)/shard_map/late_outputs/pallas_call | solution.py:114
  239.7 0.7 fusion.2
  240.5 1.0 fusion.1
  241.4 0.7 slice_bitcast_fusion.1
  242.2 0.6 reshape.104
  243.4 0.6 pad_maximum_fusion
  244.6 0.6 concatenate.24
  245.2 0.6 concatenate.23
  (40 shorter events, 3.3 us)
Async XLA Ops:
  0.6 8.6 %copy-start = (bf16[5000,256]{1,0:T(8,128)(2,1)S(1)}, bf16[5000,256]{1,0:T(8,128)(2,1)}, u32[]{:S(2)}) copy-start(bf16[5000,256]{1,0:T(8,128)(2,1)} %param.22) | copy-start | bytes 7680004
  0.7 14.3 %all-to-all-start = ((bf16[4,256,256]{2,1,0:T(8,128)(2,1)}), bf16[4,256,256]{2,1,0:T(8,128)(2,1)S(1)}, u32[]{:S(2)}, u32[]{:S(2)}) async-start(bf16[4,256,256]{2,1,0:T(8,128)(2,1)} %bitcast.55), calls=%async_computation | async-start | bytes 1048576 | tf_op jit(solution)/shard_map/all_to_all | solution.py:584
  14.9 0.8 copy-start.5
  52.2 3.7 %copy-start.11 = (bf16[224,256]{1,0:T(8,128)(2,1)S(1)}, bf16[224,256]{1,0:T(8,128)(2,1)}, u32[]{:S(2)}) copy-start(bf16[224,256]{1,0:T(8,128)(2,1)} %get-tuple-element.68.swap_ref) | copy-start | bytes 344068
  52.2 3.8 %copy-start.13 = (s32[1,1,128]{2,1,0:T(1,128)S(1)}, s32[1,1,128]{2,1,0:T(1,128)}, u32[]{:S(2)}) copy-start(s32[1,1,128]{2,1,0:T(1,128)} %param.19) | copy-start | bytes 1540
  53.7 5.6 %collective-permute-start.1 = (bf16[2560,256]{1,0:T(8,128)(2,1)S(1)}, bf16[2560,256]{1,0:T(8,128)(2,1)S(1)}, u32[]{:S(2)}, u32[]{:S(2)}) collective-permute-start(bf16[2560,256]{1,0:T(8,128)(2,1)S(1)} %dynamic-slice_bitcast_fusion.1), channel_id=1, source_target_pairs={{0,1},{1,0},{2,3},{3,2},{4,5},{5,4},{6,7},{7,6},{8,9},{9,8},{10,11... | collective-permute-start | bytes 3932168 | tf_op jit(solution)/shard_map/ppermute | solution.py:560
  55.9 3.4 %collective-permute-start.2 = (bf16[224,256]{1,0:T(8,128)(2,1)S(1)}, bf16[224,256]{1,0:T(8,128)(2,1)S(1)}, u32[]{:S(2)}, u32[]{:S(2)}) collective-permute-start(bf16[224,256]{1,0:T(8,128)(2,1)S(1)} %copy-done.11), channel_id=1, source_target_pairs={{0,1},{1,0},{2,3},{3,2},{4,5},{5,4},{6,7},{7,6},{8,9},{9,8},{10,11... | collective-permute-start | bytes 344072 | tf_op jit(solution)/shard_map/ppermute | solution.py:560
  56.0 2.7 %collective-permute-start = (s32[128]{0:T(128)S(1)}, s32[128]{0:T(128)S(1)}, u32[]{:S(2)}, u32[]{:S(2)}) collective-permute-start(s32[128]{0:T(128)S(1)} %bitcast.63), channel_id=1, source_target_pairs={{0,1},{1,0},{2,3},{3,2},{4,5},{5,4},{6,7},{7,6},{8,9},{9,8},{10,11... | collective-permute-start | bytes 1544 | tf_op jit(solution)/shard_map/ppermute | solution.py:560
  59.3 0.6 copy-start.12
  59.3 1.1 copy-start.4
  64.8 51.8 %all-to-all-start.1 = ((bf16[64,80,256]{2,1,0:T(8,128)(2,1)}), bf16[64,80,256]{2,1,0:T(8,128)(2,1)}, u32[]{:S(2)}, u32[]{:S(2)}) async-start(bf16[64,80,256]{2,1,0:T(8,128)(2,1)} %bitcast.45), calls=%async_computation.1 | async-start | bytes 5242880 | tf_op jit(solution)/shard_map/all_to_all | solution.py:649
  92.5 24.1 %collective-permute-start.3 = (bf16[2656,256]{1,0:T(8,128)(2,1)S(1)}, bf16[2656,256]{1,0:T(8,128)(2,1)}, u32[]{:S(2)}, u32[]{:S(2)}) collective-permute-start(bf16[2656,256]{1,0:T(8,128)(2,1)S(1)} %dynamic-slice_bitcast_fusion), channel_id=1, source_target_pairs={{0,1},{1,0},{2,3},{3,2},{4,5},{5,4},{6,7},{7,6},{8,9},{9,8},{10,11... | collective-permute-start | bytes 4079624 | tf_op jit(solution)/shard_map/ppermute | solution.py:560
  115.1 1.5 collective-permute-start.4
  116.6 0.7 copy-start.7
  122.9 10.5 %copy-start.6 = (bf16[1024,256]{1,0:T(8,128)(2,1)S(1)}, bf16[1024,256]{1,0:T(8,128)(2,1)}, u32[]{:S(2)}) copy-start(bf16[1024,256]{1,0:T(8,128)(2,1)} %get-tuple-element.81) | copy-start | bytes 1572868
  122.9 65.4 %all-to-all-start.2 = ((bf16[64,128,256]{2,1,0:T(8,128)(2,1)}), bf16[64,128,256]{2,1,0:T(8,128)(2,1)}, u32[]{:S(2)}, u32[]{:S(2)}) async-start(bf16[64,128,256]{2,1,0:T(8,128)(2,1)} %late_merge.1), calls=%async_computation.2 | async-start | bytes 8388608 | tf_op jit(solution)/shard_map/all_to_all | solution.py:688
  134.1 36.0 %collective-permute-start.7 = (bf16[256,256]{1,0:T(8,128)(2,1)S(1)}, bf16[256,256]{1,0:T(8,128)(2,1)S(1)}, u32[]{:S(2)}, u32[]{:S(2)}) collective-permute-start(bf16[256,256]{1,0:T(8,128)(2,1)S(1)} %get-tuple-element.99), channel_id=1, source_target_pairs={{0,96},{32,0},{64,32},{96,64},{1,97},{33,1},{65,33},{97,65},{2,98}... | collective-permute-start | bytes 393224 | tf_op jit(solution)/shard_map/ppermute | solution.py:695
  136.2 33.9 %collective-permute-start.6 = (bf16[256,256]{1,0:T(8,128)(2,1)S(1)}, bf16[256,256]{1,0:T(8,128)(2,1)S(1)}, u32[]{:S(2)}, u32[]{:S(2)}) collective-permute-start(bf16[256,256]{1,0:T(8,128)(2,1)S(1)} %get-tuple-element.100), channel_id=1, source_target_pairs={{0,64},{32,96},{64,0},{96,32},{1,65},{33,97},{65,1},{97,33},{2,66}... | collective-permute-start | bytes 393224 | tf_op jit(solution)/shard_map/ppermute | solution.py:695
  136.6 48.9 %collective-permute-start.5 = (bf16[256,256]{1,0:T(8,128)(2,1)S(1)}, bf16[256,256]{1,0:T(8,128)(2,1)S(1)}, u32[]{:S(2)}, u32[]{:S(2)}) collective-permute-start(bf16[256,256]{1,0:T(8,128)(2,1)S(1)} %get-tuple-element.101), channel_id=1, source_target_pairs={{0,32},{32,64},{64,96},{96,0},{1,33},{33,65},{65,97},{97,1},{2,34}... | collective-permute-start | bytes 393224 | tf_op jit(solution)/shard_map/ppermute | solution.py:695
  170.1 15.4 %copy-start.8 = (bf16[256,256]{1,0:T(8,128)(2,1)}, bf16[256,256]{1,0:T(8,128)(2,1)S(1)}, u32[]{:S(2)}) copy-start(bf16[256,256]{1,0:T(8,128)(2,1)S(1)} %collective-permute-done.7.third_ref) | copy-start | bytes 393220
  170.1 15.4 %copy-start.9 = (bf16[256,256]{1,0:T(8,128)(2,1)}, bf16[256,256]{1,0:T(8,128)(2,1)S(1)}, u32[]{:S(2)}) copy-start(bf16[256,256]{1,0:T(8,128)(2,1)S(1)} %collective-permute-done.6.second_ref) | copy-start | bytes 393220
  185.5 0.7 copy-start.10
  192.7 12.3 %collective-permute-start.8 = (bf16[5120,256]{1,0:T(8,128)(2,1)}, bf16[5120,256]{1,0:T(8,128)(2,1)}, u32[]{:S(2)}, u32[]{:S(2)}) collective-permute-start(bf16[5120,256]{1,0:T(8,128)(2,1)} %bitcast.50), channel_id=1, source_target_pairs={{0,1},{1,0},{2,3},{3,2},{4,5},{5,4},{6,7},{7,6},{8,9},{9,8},{10,11... | collective-permute-start | bytes 7864328 | tf_op jit(solution)/shard_map/ppermute | solution.py:560
  193.7 34.2 %all-to-all-start.3 = ((bf16[64,48,256]{2,1,0:T(8,128)(2,1)}), bf16[64,48,256]{2,1,0:T(8,128)(2,1)S(1)}, u32[]{:S(2)}, u32[]{:S(2)}) async-start(bf16[64,48,256]{2,1,0:T(8,128)(2,1)} %get-tuple-element.86), calls=%async_computation.3 | async-start | bytes 3145728 | tf_op jit(solution)/shard_map/all_to_all | solution.py:708
  227.8 1.2 copy-start.2
  229.0 4.7 %collective-permute-start.9 = (bf16[3072,256]{1,0:T(8,128)(2,1)S(1)}, bf16[3072,256]{1,0:T(8,128)(2,1)S(1)}, u32[]{:S(2)}, u32[]{:S(2)}) collective-permute-start(bf16[3072,256]{1,0:T(8,128)(2,1)S(1)} %bitcast.46), channel_id=1, source_target_pairs={{0,1},{1,0},{2,3},{3,2},{4,5},{5,4},{6,7},{7,6},{8,9},{9,8},{10,11... | collective-permute-start | bytes 4718600 | tf_op jit(solution)/shard_map/ppermute | solution.py:560
  233.6 1.2 copy-start.3
  234.8 11.0 %copy-start.1 = (bf16[5000,256]{1,0:T(8,128)(2,1)S(1)}, bf16[5000,256]{1,0:T(8,128)(2,1)}, u32[]{:S(2)}) copy-start(bf16[5000,256]{1,0:T(8,128)(2,1)} %param.22) | copy-start | bytes 7680004
